TPU v7x, 256 devices: a whole 4x4x8 slice. The times are simulated.
256 devices in a mesh: section: 16 (over y, z_hi), tp: 16 (over x, z_lo, core).
Axes of the slice: x: 4, y: 4, z: 8 (z_hi: 4, z_lo: 2; z = z_hi * 2 + z_lo), core: 2. Of those that a mesh axis runs over, the one named last changes fastest.
Arguments:
- saved_in: bfloat16 [16, 1024, 3072], P('section', 'tp'), may hold values from -6 to 6
- out_grad: bfloat16 [16, 1024, 3072], P('section', 'tp'), may hold values from -6 to 6
- pending: bfloat16 [16, 1024, 3072], P('section', 'tp'), may hold values from -6 to 6
- gain: float32 [16, 3072], P('section'), may hold values from 0.5 to 1.5
- alpha: float32 [16, 16], replicated, may hold values from 0.2 to 1
- w_query: bfloat16 [16, 3072, 4096], P('section', None, 'tp'), may hold values from -0.5 to 0.5
- w_key: bfloat16 [16, 3072, 4096], P('section', None, 'tp'), may hold values from -0.5 to 0.5
- w_value: bfloat16 [16, 3072, 4096], P('section', None, 'tp'), may hold values from -0.109375 to 0.109375
- w_out: bfloat16 [16, 4096, 3072], P('section', 'tp'), may hold values from -0.09375 to 0.09375
Outputs:
- in_grads: bfloat16 [16, 1024, 3072], P('section', 'tp')
- new_pending: bfloat16 [16, 1024, 3072], P('section', 'tp')
All inputs are finite; a program needn't handle non-finite values.
Results may differ from a plain program's by a relative error of at most 0.029.
Values may be sent and summed in bfloat16 or wider, within the bound.
A program may use at most 256 MiB of HBM per device.

v0:
```python
import math

import jax
import jax.numpy as jnp
from jax import lax
from jax.sharding import PartitionSpec as P

HEAD = 128


eps = 1e-05


def normalize(rows, gain_row):
    values = rows.astype(jnp.float32)
    factor = lax.rsqrt(jnp.mean(values * values, axis=-1, keepdims=True) + eps)
    return (values * factor * gain_row).astype(jnp.bfloat16)


def project_rows(rows, gain_row, query_weight, key_weight, value_weight):
    normed = normalize(rows, gain_row)
    query = jnp.dot(normed, query_weight, preferred_element_type=jnp.float32).astype(jnp.bfloat16)
    keys = jnp.dot(normed, key_weight, preferred_element_type=jnp.float32).astype(jnp.bfloat16)
    values = jnp.dot(normed, value_weight, preferred_element_type=jnp.float32).astype(jnp.bfloat16)
    return jnp.concatenate((query, keys, values), axis=1)


def heads_back(grad_rows, out_weight):
    product = jnp.einsum("td,ed->te", grad_rows, out_weight, preferred_element_type=jnp.float32)
    return product.astype(jnp.bfloat16)


def attend_back(query, keys, values, grad_heads):
    tokens = query.shape[0]
    heads = query.shape[1] // HEAD
    shape = (tokens, heads, HEAD)
    query = query.reshape(shape)
    keys = keys.reshape(shape)
    values = values.reshape(shape)
    grad_heads = grad_heads.reshape(shape)
    scale = 1.0 / math.sqrt(HEAD)
    scores = jnp.einsum("qhe,khe->hqk", query, keys, preferred_element_type=jnp.float32) * scale
    causal = jnp.arange(tokens)[:, None] >= jnp.arange(tokens)[None, :]
    scores = jnp.where(causal[None], scores, -1e30)
    peak = jnp.max(scores, axis=-1, keepdims=True)
    weights = jnp.exp(scores - peak)
    weights = weights / jnp.sum(weights, axis=-1, keepdims=True)
    probs = weights.astype(jnp.bfloat16)
    output = jnp.einsum("hqk,khe->hqe", probs, values, preferred_element_type=jnp.float32)
    delta = jnp.einsum("qhe,hqe->hq", grad_heads.astype(jnp.float32), output)[:, :, None]
    grad_probs = jnp.einsum("qhe,khe->hqk", grad_heads, values, preferred_element_type=jnp.float32)
    grad_scores = (weights * (grad_probs - delta) * scale).astype(jnp.bfloat16)
    grad_query = jnp.einsum(
        "hqk,khe->qhe", grad_scores, keys, preferred_element_type=jnp.float32
    ).astype(jnp.bfloat16)
    grad_keys = jnp.einsum(
        "hqk,qhe->khe", grad_scores, query, preferred_element_type=jnp.float32
    ).astype(jnp.bfloat16)
    grad_values = jnp.einsum(
        "hqk,qhe->khe", probs, grad_heads, preferred_element_type=jnp.float32
    ).astype(jnp.bfloat16)
    flat = (tokens, heads * HEAD)
    return (grad_query.reshape(flat), grad_keys.reshape(flat), grad_values.reshape(flat))


def on_device(saved_in, out_grad, pending, gain, alpha, w_query, w_key, w_value, w_out):
    saved_rows = saved_in[0]
    grad_rows = out_grad[0]
    gain_row = gain[0]
    query_weight = w_query[0]
    key_weight = w_key[0]
    value_weight = w_value[0]
    out_weight = w_out[0]
    width = query_weight.shape[1]
    all_saved, all_grads = (
        lax.all_gather(saved_rows, "tp", axis=0, tiled=True),
        lax.all_gather(grad_rows, "tp", axis=0, tiled=True),
    )
    projected = project_rows(all_saved, gain_row, query_weight, key_weight, value_weight)
    grad_heads = heads_back(all_grads, out_weight)
    query = projected[:, :width]
    keys = projected[:, width : 2 * width]
    values = projected[:, 2 * width :]
    grad_query, grad_keys, grad_values = attend_back(query, keys, values, grad_heads)
    rows = saved_rows.shape[0]
    total = jnp.zeros((lax.axis_size("tp") * rows, out_weight.shape[1]), jnp.float32)
    for grad_part, weight in (
        (grad_query, query_weight),
        (grad_keys, key_weight),
        (grad_values, value_weight),
    ):
        total = total + jnp.einsum(
            "te,de->td", grad_part, weight, preferred_element_type=jnp.float32
        )
    grad_normed = lax.psum_scatter(
        total.astype(jnp.bfloat16), "tp", scatter_dimension=0, tiled=True
    ).astype(jnp.float32)
    saved_float = saved_rows.astype(jnp.float32)
    factor = lax.rsqrt(jnp.mean(saved_float * saved_float, axis=-1, keepdims=True) + eps)
    scaled = grad_normed * gain_row
    inner = jnp.mean(scaled * saved_float, axis=-1, keepdims=True)
    grad_input = (
        grad_rows.astype(jnp.float32) + factor * (scaled - saved_float * factor * factor * inner)
    ).astype(jnp.bfloat16)
    sections = lax.axis_size("section")
    place = lax.axis_index("section")
    slot_ids = jnp.arange(sections, dtype=jnp.int32)
    arrived = lax.all_gather(grad_input[None], "section", axis=0, tiled=True)
    column = lax.dynamic_slice_in_dim(alpha, place, 1, 1)[:, 0]
    coeffs = jnp.where(slot_ids > place, column, 0.0)

    def add_one(source, total):
        return total + coeffs[source] * arrived[source].astype(jnp.float32)

    updated = lax.fori_loop(0, sections, add_one, pending[0].astype(jnp.float32)).astype(
        jnp.bfloat16
    )
    return (grad_input[None], updated[None])


def solution(mesh):
    return jax.shard_map(
        on_device,
        mesh=mesh,
        in_specs=(
            P("section", "tp", None),
            P("section", "tp", None),
            P("section", "tp", None),
            P("section", None),
            P(),
            P("section", None, "tp"),
            P("section", None, "tp"),
            P("section", None, "tp"),
            P("section", "tp", None),
        ),
        out_specs=(P("section", "tp", None), P("section", "tp", None)),
        check_vma=False,
    )
```

profile of v0, /device:TPU:8, one launch (start us, length us, event | category | flops | bytes accessed | tf_op | source)
XLA Modules:
  0.0 399.9 jit_solution(3184886904353822880)
XLA Ops:
  10.0 47.7 %all-gather.7.cloned.1.call-done = bf16[1,1024,3072]{2,1,0:T(8,128)(2,1)} async-done(((bf16[1,64,3072]{2,1,0:T(8,128)(2,1)}), bf16[1,1024,3072]{2,1,0:T(8,128)(2,1)}) %all-gather.7.cloned.1.call-update) | async-done | bytes 6291472 | tf_op jit(solution)/shard_map/all_gather | solution.py:76
  57.7 4.1 %fusion.1 = f32[1024]{0:T(1024)S(1)} fusion(bf16[1,1024,3072]{2,1,0:T(8,128)(2,1)} %all-gather.7.cloned.1.call-done), kind=kLoop, calls=%fused_computation.4 | loop fusion | flops 9436160 | bytes 6295552 | tf_op jit(solution)/shard_map/reduce_sum | solution.py:16
  61.8 43.5 %all-gather.9.cloned.1.call-done = bf16[1,1024,3072]{2,1,0:T(8,128)(2,1)} async-done(((bf16[1,64,3072]{2,1,0:T(8,128)(2,1)}), bf16[1,1024,3072]{2,1,0:T(8,128)(2,1)}) %all-gather.9.cloned.1.call-update) | async-done | bytes 6291472 | tf_op jit(solution)/shard_map/all_gather | solution.py:77
  105.3 5.0 %fusion.32 = bf16[1024,256]{0,1:T(8,128)(2,1)S(1)} fusion(bf16[1,256,3072]{2,1,0:T(8,128)(2,1)} %param.19, bf16[1,1024,3072]{2,1,0:T(8,128)(2,1)} %all-gather.9.cloned.1.call-done), kind=kOutput, calls=%fused_computation.36 | convolution fusion | flops 1610874880 | bytes 8388608 | tf_op jit(solution)/shard_map/td,ed->te/dot_general | solution.py:29
  110.5 6.1 %fusion.26 = bf16[1024,256]{0,1:T(8,128)(2,1)} fusion(bf16[1,3072,256]{2,1,0:T(8,128)(2,1)} %param.16, bf16[1,1024,3072]{2,1,0:T(8,128)(2,1)} %all-gather.7.cloned.1.call-done, f32[3072]{0:T(1024)S(1)} %bitcast.109, f32[1024]{0:T(1024)S(1)} %add_rsqrt_fusion), kind=kOutput, calls=%fused_computation.34 | convolution fusion | flops 1623457792 | bytes 8404992 | tf_op jit(solution)/shard_map/dot_general | solution.py:22
  116.7 5.7 %fusion.23 = bf16[1024,256]{0,1:T(8,128)(2,1)} fusion(bf16[1,3072,256]{2,1,0:T(8,128)(2,1)S(1)} %copy-done, bf16[1,1024,3072]{2,1,0:T(8,128)(2,1)} %all-gather.7.cloned.1.call-done, f32[3072]{0:T(1024)S(1)} %bitcast.110, f32[1024]{0:T(1024)S(1)} %add_rsqrt_fusion), kind=kOutput, calls=%fused_computation.33 | convolution fusion | flops 1623457792 | bytes 8404992 | tf_op jit(solution)/shard_map/dot_general | solution.py:23
  122.4 8.1 %fusion.53 = (f32[2,1024]{1,0:T(2,128)S(1)}, f32[2,1024,1024]{1,2,0:T(8,128)}) fusion(pred[1024,1024]{0,1:T(8,128)(4,1)} %iota_compare_fusion, bf16[1024,2,128]{0,2,1:T(8,128)(2,1)} %bitcast.105, bf16[1024,2,128]{0,2,1:T(8,128)(2,1)} %bitcast.103), kind=kOutput, calls=%fused_computation.63 | convolution fusion | flops 545260544 | bytes 10493952 | tf_op jit(solution)/shard_map/sub | solution.py:46
  130.5 5.0 %fusion.10 = bf16[2,1024,1024]{1,2,0:T(8,128)(2,1)S(1)} fusion(f32[2,1024,1024]{1,2,0:T(8,128)} %get-tuple-element.93, f32[2,1024]{1,0:T(2,128)S(1)} %get-tuple-element.92), kind=kLoop, calls=%fused_computation.19 | loop fusion | flops 4194304 | bytes 12591104 | tf_op jit(solution)/shard_map/convert_element_type | solution.py:48
  135.5 5.1 %fusion.29 = bf16[1024,256]{0,1:T(8,128)(2,1)S(1)} fusion(bf16[1,3072,256]{2,1,0:T(8,128)(2,1)S(1)} %copy-done.2, bf16[1,1024,3072]{2,1,0:T(8,128)(2,1)} %all-gather.7.cloned.1.call-done, f32[3072]{0:T(1024)S(1)} %bitcast.111, f32[1024]{0:T(1024)S(1)} %add_rsqrt_fusion), kind=kOutput, calls=%fused_computation.35 | convolution fusion | flops 1623457792 | bytes 8404992 | tf_op jit(solution)/shard_map/dot_general | solution.py:24
  140.7 2.0 fusion.37
  148.4 6.3 %fusion.19 = f32[1024,3072]{1,0:T(8,128)} fusion(bf16[1024,256]{0,1:T(8,128)(2,1)S(1)} %bitcast.99, bf16[1,3072,256]{2,1,0:T(8,128)(2,1)S(1)} %copy-done), kind=kOutput, calls=%fused_computation.28 | convolution fusion | flops 1610612736 | bytes 14680064 | tf_op jit(solution)/shard_map/te,de->td/dot_general | solution.py:92
  154.7 6.4 %fusion.15 = f32[1024,3072]{1,0:T(8,128)} fusion(bf16[1024,256]{0,1:T(8,128)(2,1)S(1)} %bitcast.100, bf16[1,3072,256]{2,1,0:T(8,128)(2,1)S(1)} %copy-done.3), kind=kOutput, calls=%fused_computation.24 | convolution fusion | flops 1610612736 | bytes 14680064 | tf_op jit(solution)/shard_map/te,de->td/dot_general | solution.py:92
  161.1 12.1 %add_convert_fusion = bf16[1024,3072]{1,0:T(8,128)(2,1)} fusion(f32[1024,3072]{1,0:T(8,128)} %fusion.15, f32[1024,3072]{1,0:T(8,128)} %fusion.19, bf16[1024,256]{0,1:T(8,128)(2,1)S(1)} %bitcast.95, bf16[1,3072,256]{2,1,0:T(8,128)(2,1)S(1)} %copy-done.2), kind=kOutput, calls=%fused_computation.7 | convolution fusion | flops 1620049920 | bytes 33554432 | tf_op jit(solution)/shard_map/te,de->td/dot_general | solution.py:92
  173.3 81.3 %reduce-scatter.2.cloned.1.call-done = bf16[64,3072]{1,0:T(8,128)(2,1)} async-done(((bf16[1024,3072]{1,0:T(8,128)(2,1)}), bf16[64,3072]{1,0:T(8,128)(2,1)}) %reduce-scatter.2.cloned.1.call-update) | async-done | bytes 393232 | tf_op jit(solution)/shard_map/reduce_scatter | solution.py:95
  255.9 2.1 fusion.46
  258.2 95.2 %all-gather.11.cloned.1.call-done = bf16[1024,3072]{1,0:T(8,128)(2,1)} async-done(((bf16[64,3072]{1,0:T(8,128)(2,1)}), bf16[1024,3072]{1,0:T(8,128)(2,1)}) %all-gather.11.cloned.1.call-update) | async-done | bytes 6291472 | tf_op jit(solution)/shard_map/all_gather | solution.py:108
  353.4 39.1 %while.13 = (s32[]{:T(128)}, f32[64,3072]{1,0:T(8,128)S(1)}, f32[16]{0:T(128)S(1)}, bf16[16,64,3072]{2,1,0:T(8,128)(2,1)}, s32[]{:T(128)}) while((s32[]{:T(128)}, f32[64,3072]{1,0:T(8,128)S(1)}, f32[16]{0:T(128)S(1)}, bf16[16,64,3072]{2,1,0:T(8,128)(2,1)}, s32[]{:T(128)}) %tuple.46), condition=%wide.region_7.8_spmd, body=%wide.region_6.7_spmd.sunk | while | flops 589826 | bytes 1966161 | solution.py:115
  354.0 1.8 bitcast_add_fusion.2
  356.5 1.8 bitcast_add_fusion.2
  358.9 1.8 bitcast_add_fusion.2
  361.4 1.8 bitcast_add_fusion.2
  363.8 1.8 bitcast_add_fusion.2
  366.2 1.8 bitcast_add_fusion.2
  368.7 1.8 bitcast_add_fusion.2
  371.1 1.8 bitcast_add_fusion.2
  373.6 1.8 bitcast_add_fusion.2
  376.0 1.8 bitcast_add_fusion.2
  378.5 1.8 bitcast_add_fusion.2
  380.9 1.8 bitcast_add_fusion.2
  383.4 1.8 bitcast_add_fusion.2
  388.3 1.8 bitcast_add_fusion.2
  390.7 1.8 bitcast_add_fusion.2
  (63 shorter events, 22.6 us)
Async XLA Ops:
  7.2 109.5 %copy-start = (bf16[1,3072,256]{2,1,0:T(8,128)(2,1)S(1)}, bf16[1,3072,256]{2,1,0:T(8,128)(2,1)}, u32[]{:S(2)}) copy-start(bf16[1,3072,256]{2,1,0:T(8,128)(2,1)} %param.17) | copy-start | bytes 4718596
  7.2 50.5 %all-gather.7.cloned.1.call-start = ((), (), s32[]{:S(2)}) async-start(), calls=%async_computation.2 | async-start | bytes 6684672 | tf_op jit(solution)/shard_map/all_gather | solution.py:76
  7.9 97.4 %all-gather.9.cloned.1.call-start = ((), (), s32[]{:S(2)}) async-start(), calls=%async_computation.3 | async-start | bytes 6684672 | tf_op jit(solution)/shard_map/all_gather | solution.py:77
  8.7 245.9 %reduce-scatter.2.cloned.1.call-start = ((), (), s32[]{:S(2)}) async-start(), calls=%async_computation.1 | async-start | bytes 6684672 | tf_op jit(solution)/shard_map/reduce_scatter | solution.py:95
  61.8 48.8 %copy-start.8 = (f32[1,3072]{1,0:T(1,128)S(1)}, f32[1,3072]{1,0:T(1,128)}, u32[]{:S(2)}) copy-start(f32[1,3072]{1,0:T(1,128)} %param.14) | copy-start | bytes 36868
  130.5 5.0 %copy-start.2 = (bf16[1,3072,256]{2,1,0:T(8,128)(2,1)S(1)}, bf16[1,3072,256]{2,1,0:T(8,128)(2,1)}, u32[]{:S(2)}) copy-start(bf16[1,3072,256]{2,1,0:T(8,128)(2,1)} %param.18) | copy-start | bytes 4718596
  130.5 12.1 %slice-start = ((s8[8388608]{0:T(1024)(128)(4,1)}), s8[4194304]{0:T(1024)(128)(4,1)S(1)}, s32[]{:S(2)}) async-start(s8[8388608]{0:T(1024)(128)(4,1)} %bitcast.93), calls=%async_computation.5 | async-start | bytes 8388608
  135.5 7.1 %slice-start.1 = ((s8[8388608]{0:T(1024)(128)(4,1)}), s8[4194304]{0:T(1024)(128)(4,1)S(1)}, s32[]{:S(2)}) async-start(s8[8388608]{0:T(1024)(128)(4,1)} %bitcast.93), calls=%async_computation.6 | async-start | bytes 8388608
  142.7 1.8 copy-start.6
  142.7 3.4 copy-start.5
  148.3 6.4 %copy-start.3 = (bf16[1,3072,256]{2,1,0:T(8,128)(2,1)S(1)}, bf16[1,3072,256]{2,1,0:T(8,128)(2,1)}, u32[]{:S(2)}) copy-start(bf16[1,3072,256]{2,1,0:T(8,128)(2,1)} %param.16) | copy-start | bytes 4718596
  173.2 81.4 %copy-start.1 = (bf16[1,64,3072]{2,1,0:T(8,128)(2,1)S(1)}, bf16[1,64,3072]{2,1,0:T(8,128)(2,1)}, u32[]{:S(2)}) copy-start(bf16[1,64,3072]{2,1,0:T(8,128)(2,1)} %param.11) | copy-start | bytes 1179652
  173.2 82.7 %copy-start.4 = (bf16[1,64,3072]{2,1,0:T(8,128)(2,1)S(1)}, bf16[1,64,3072]{2,1,0:T(8,128)(2,1)}, u32[]{:S(2)}) copy-start(bf16[1,64,3072]{2,1,0:T(8,128)(2,1)} %param.12) | copy-start | bytes 1179652
  173.2 84.8 %copy-start.9 = (f32[16,16]{1,0:T(8,128)S(1)}, f32[16,16]{1,0:T(8,128)}, u32[]{:S(2)}) copy-start(f32[16,16]{1,0:T(8,128)} %param.15) | copy-start | bytes 3076
  173.2 85.0 %copy-start.7 = (bf16[1,64,3072]{2,1,0:T(8,128)(2,1)S(1)}, bf16[1,64,3072]{2,1,0:T(8,128)(2,1)}, u32[]{:S(2)}) copy-start(bf16[1,64,3072]{2,1,0:T(8,128)(2,1)} %param.13) | copy-start | bytes 1179652
  173.2 180.2 %all-gather.11.cloned.1.call-start = ((), (), s32[]{:S(2)}) async-start(), calls=%async_computation.4 | async-start | bytes 6684672 | tf_op jit(solution)/shard_map/all_gather | solution.py:108
Sparse Core Ops, SparseCore 0:
  9.9 47.7 all-gather.6
  59.5 45.6 all-gather.8
  173.4 81.1 reduce-scatter.1
  258.1 95.2 all-gather.10
where the time goes:
time: 401 us; the launch traced here: 400 us
  waiting for transfers between devices  269 us (67%)
  matrix products  62.5 us (16%)
  other arithmetic  43.7 us (11%)
  between operations  14 us (3%)
  local copies, waits for them, and re-layouts  10.2 us (3%)
    all_gather x1, waiting for transfers between devices, on_device(): arrived = lax.all_gather(grad_input[None], 'section', axis=0, tiled=True)  95.2 us
    reduce_scatter x1, waiting for transfers between devices, on_device(): lax.psum_scatter(total.astype(jnp.bfloat16), 'tp', scatter_dimension=0, t...  81.3 us
    all_gather x1, waiting for transfers between devices, on_device(): lax.all_gather(saved_rows, 'tp', axis=0, tiled=True)  47.7 us
    all_gather x1, waiting for transfers between devices, on_device(): lax.all_gather(grad_rows, 'tp', axis=0, tiled=True)  43.5 us
    add x16, other arithmetic, add_one(): return total + coeffs[source] * arrived[source].astype(jnp.float32)  29.1 us
    dot_general x3, matrix products, on_device(): jnp.einsum('te,de->td', grad_part, weight, preferred_element_type=jnp.flo...  24.8 us
    dynamic_slice x16, local copies, waits for them, and re-layouts, add_one(): return total + coeffs[source] * arrived[source].astype(jnp.float32)  9.73 us
    sub x1, matrix products, attend_back(): weights = jnp.exp(scores - peak)  8.15 us
  transfers between devices with their start and end apart: 4, of which 4 were waited for; matrix products, arithmetic and copies ran while one was open for 1% of the time, Pallas kernels for 0%

commit v1 on v0

v1 whole, which is shorter than its diff:
```python
import functools
import math

import jax
import jax.numpy as jnp
from jax import lax
from jax.experimental import pallas as pl
from jax.experimental.pallas import tpu as pltpu
from jax.sharding import PartitionSpec as P

HEAD = 128
MESH = pl.DeviceIdType.MESH

eps = 1e-05


def normalize(rows, gain_row):
    values = rows.astype(jnp.float32)
    factor = lax.rsqrt(jnp.mean(values * values, axis=-1, keepdims=True) + eps)
    return (values * factor * gain_row).astype(jnp.bfloat16)


def project_rows(rows, gain_row, query_weight, key_weight, value_weight):
    normed = normalize(rows, gain_row)
    query = jnp.dot(normed, query_weight, preferred_element_type=jnp.float32).astype(jnp.bfloat16)
    keys = jnp.dot(normed, key_weight, preferred_element_type=jnp.float32).astype(jnp.bfloat16)
    values = jnp.dot(normed, value_weight, preferred_element_type=jnp.float32).astype(jnp.bfloat16)
    return query, keys, values


def heads_back(grad_rows, out_weight):
    product = jnp.einsum("td,ed->te", grad_rows, out_weight, preferred_element_type=jnp.float32)
    return product.astype(jnp.bfloat16)


def dot(a, b, ca, cb):
    return lax.dot_general(a, b, (((ca,), (cb,)), ((), ())), preferred_element_type=jnp.float32)


def attend_kernel(q_ref, k_ref, v_ref, g_ref, dq_ref, dk_ref, dv_ref, dk_acc, dv_acc, *, block):
    tokens, width = q_ref.shape
    scale = 1.0 / math.sqrt(HEAD)
    log2e = math.log2(math.e)
    below = lax.broadcasted_iota(jnp.int32, (block, block), 0) <= lax.broadcasted_iota(
        jnp.int32, (block, block), 1
    )
    for head in range(width // HEAD):
        cols = pl.ds(head * HEAD, HEAD)
        keys_t = k_ref[:, cols].T
        values_t = v_ref[:, cols].T
        for step in reversed(range(tokens // block)):
            n = (step + 1) * block
            rows = pl.ds(step * block, block)
            query, grad = q_ref[rows, cols], g_ref[rows, cols]
            scores = dot(k_ref[pl.ds(0, n), cols], query, 1, 1) * (scale * log2e)
            last = jnp.where(below, scores[n - block :], -1e30)
            scores = last if step == 0 else jnp.concatenate((scores[: n - block], last), axis=0)
            peak = jnp.max(scores, axis=0, keepdims=True)
            weights = jnp.exp2(scores - peak)
            weights = weights * (1.0 / jnp.sum(weights, axis=0, keepdims=True))
            probs = weights.astype(jnp.bfloat16)
            output_t = dot(values_t[:, :n], probs, 1, 0)
            grad_t = grad.astype(jnp.float32).T
            delta = jnp.sum(grad_t * output_t, axis=0, keepdims=True)
            grad_probs = dot(v_ref[pl.ds(0, n), cols], grad, 1, 1)
            grad_scores = (weights * ((grad_probs - delta) * scale)).astype(jnp.bfloat16)
            dq_ref[rows, cols] = dot(keys_t[:, :n], grad_scores, 1, 0).T.astype(jnp.bfloat16)
            more_k = dot(grad_scores, query, 1, 0)
            more_v = dot(probs, grad, 1, 0)
            if step == tokens // block - 1:
                dk_acc[...] = more_k
                dv_acc[...] = more_v
            else:
                dk_acc[pl.ds(0, n)] += more_k
                dv_acc[pl.ds(0, n)] += more_v
        dk_ref[:, cols] = dk_acc[...].astype(jnp.bfloat16)
        dv_ref[:, cols] = dv_acc[...].astype(jnp.bfloat16)


def attend_back(query, keys, values, grad_heads):
    tokens, width = query.shape
    out = jax.ShapeDtypeStruct((tokens, width), jnp.bfloat16)
    whole = pl.BlockSpec(memory_space=pltpu.VMEM)
    return pl.pallas_call(
        functools.partial(attend_kernel, block=256),
        out_shape=(out, out, out),
        in_specs=[whole] * 4,
        out_specs=(whole,) * 3,
        scratch_shapes=[pltpu.VMEM((tokens, HEAD), jnp.float32)] * 2,
        compiler_params=pltpu.CompilerParams(vmem_limit_bytes=40 * 2**20),
        cost_estimate=pl.CostEstimate(flops=2 * 10**9, bytes_accessed=4 * 10**6, transcendentals=10**6),
    )(query, keys, values, grad_heads)


def section_kernel(alpha_ref, mine_ref, pending_ref, out_ref, gather, part, stage, arrived,
                   send_sem, recv_sem, *, ny, nz):
    place = lax.axis_index("section")
    y, z = place // nz, lax.rem(place, nz)
    rows, depth = mine_ref.shape
    half, quarter = rows // 2, rows // 4
    wide = 512

    def at(dy, dz):
        return lax.rem(y + dy + ny, ny) * nz + lax.rem(z + dz + nz, nz)

    up = (at(1, 0), at(0, 1))
    down = (at(-1, 0), at(0, -1))

    barrier = pltpu.get_barrier_semaphore()
    for other in up + down:
        pl.semaphore_signal(barrier, inc=1, device_id={"section": other}, device_id_type=MESH)
    pl.semaphore_wait(barrier, 4)

    def copy(index, src, dst, to):
        return pltpu.make_async_remote_copy(
            src_ref=src, dst_ref=dst, send_sem=send_sem.at[index], recv_sem=recv_sem.at[index],
            device_id={"section": to}, device_id_type=MESH,
        )

    lo, hi = pl.ds(0, quarter), pl.ds(quarter, quarter)
    sends = []

    def go(c):
        c.start()
        sends.append(c)
        return c

    first = []
    for w in (1, 0):
        own = mine_ref.at[pl.ds(w * half, half)]
        first.append((
            w,
            go(copy(8 * w, own, gather.at[w, 1], up[w])),
            go(copy(8 * w + 1, own, gather.at[w, 3], down[w])),
        ))
    relay = {}
    for w in (0, 1):
        for which, a, b in first:
            if which == w:
                a.wait_recv()
                ra = go(copy(8 * w + 2, gather.at[w, 1, lo], gather.at[w, 2, lo], up[w]))
                b.wait_recv()
                rb = go(copy(8 * w + 3, gather.at[w, 3, hi], gather.at[w, 2, hi], down[w]))
                relay[w] = (ra, rb)
        if w == 0:
            pass

    def coefficient(j, s):
        return jnp.where(s > j, alpha_ref[s, j], 0.0)

    def combine(w, order):
        coeffs = {}
        for r in order:
            j = at(0, r) if w == 0 else at(r, 0)
            for t in range(4):
                s = at(-t, 0) if w == 0 else at(0, -t)
                coeffs[r, t] = coefficient(j, s)

        def body(i, carry):
            rr = pl.multiple_of(lax.rem(i, half // 16) * 16, 16)
            cc = pl.multiple_of((i // (half // 16)) * wide, wide)
            here, cols = pl.ds(rr, 16), pl.ds(cc, wide)
            blocks = [mine_ref[pl.ds(pl.multiple_of(w * half + rr, 16), 16), cols]]
            blocks += [gather[w, t, here, cols] for t in (1, 2, 3)]
            blocks = [b.astype(jnp.float32) for b in blocks]
            for r in order:
                total = blocks[0] * coeffs[r, 0]
                for t in (1, 2, 3):
                    total = total + blocks[t] * coeffs[r, t]
                part[w, r, here, cols] = total
                if r == 2:
                    stage[w, 2, here, cols] = total.astype(jnp.bfloat16)
            return carry

        lax.fori_loop(0, (half // 16) * (depth // wide), body, 0)

    def add_relay(w):
        def body(i, carry):
            cc = pl.multiple_of(i * wide, wide)
            cols = pl.ds(cc, wide)
            stage[w, 1, lo, cols] = (
                part[w, 1, lo, cols] + arrived[w, 2, lo, cols].astype(jnp.float32)
            ).astype(jnp.bfloat16)
            stage[w, 1, hi, cols] = part[w, 1, hi, cols].astype(jnp.bfloat16)
            stage[w, 3, lo, cols] = part[w, 3, lo, cols].astype(jnp.bfloat16)
            stage[w, 3, hi, cols] = (
                part[w, 3, hi, cols] + arrived[w, 2, hi, cols].astype(jnp.float32)
            ).astype(jnp.bfloat16)
            return carry

        lax.fori_loop(0, depth // wide, body, 0)

    def finish(w):
        def body(i, carry):
            rr = pl.multiple_of(lax.rem(i, half // 16) * 16, 16)
            cc = pl.multiple_of((i // (half // 16)) * wide, wide)
            here, cols = pl.ds(rr, 16), pl.ds(cc, wide)
            target = pl.ds(pl.multiple_of(w * half + rr, 16), 16)
            total = pending_ref[target, cols].astype(jnp.float32) + part[w, 0, here, cols]
            total = total + arrived[w, 1, here, cols].astype(jnp.float32)
            total = total + arrived[w, 3, here, cols].astype(jnp.float32)
            out_ref[target, cols] = total.astype(jnp.bfloat16)
            return carry

        lax.fori_loop(0, (half // 16) * (depth // wide), body, 0)

    second = {}
    for w in (0, 1):
        for c in relay[w]:
            c.wait_recv()
        combine(w, (0, 1, 2, 3))
        o = 1 - w
        second[w] = (
            go(copy(8 * w + 4, stage.at[w, 2, lo], arrived.at[w, 2, lo], up[o])),
            go(copy(8 * w + 5, stage.at[w, 2, hi], arrived.at[w, 2, hi], down[o])),
        )
    third = {}
    for w in (0, 1):
        for c in second[w]:
            c.wait_recv()
        add_relay(w)
        o = 1 - w
        third[w] = (
            go(copy(8 * w + 6, stage.at[w, 1], arrived.at[w, 1], up[o])),
            go(copy(8 * w + 7, stage.at[w, 3], arrived.at[w, 3], down[o])),
        )
    for w in (1, 0):
        for c in third[w]:
            c.wait_recv()
        finish(w)
    for c in sends:
        c.wait_send()


def section_sums(alpha, grad_input, pending):
    rows, depth = grad_input.shape
    half = rows // 2
    vmem = pl.BlockSpec(memory_space=pltpu.VMEM)
    return pl.pallas_call(
        functools.partial(section_kernel, ny=4, nz=4),
        out_shape=jax.ShapeDtypeStruct((rows, depth), jnp.bfloat16),
        in_specs=[pl.BlockSpec(memory_space=pltpu.SMEM), vmem, vmem],
        out_specs=vmem,
        scratch_shapes=[
            pltpu.VMEM((2, 4, half, depth), jnp.bfloat16),
            pltpu.VMEM((2, 4, half, depth), jnp.float32),
            pltpu.VMEM((2, 4, half, depth), jnp.bfloat16),
            pltpu.VMEM((2, 4, half, depth), jnp.bfloat16),
            pltpu.SemaphoreType.DMA((16,)),
            pltpu.SemaphoreType.DMA((16,)),
        ],
        compiler_params=pltpu.CompilerParams(
            collective_id=3, has_side_effects=True, vmem_limit_bytes=40 * 2**20
        ),
        cost_estimate=pl.CostEstimate(flops=10**7, bytes_accessed=10**6, transcendentals=0),
    )(alpha, grad_input, pending)


def on_device(saved_in, out_grad, pending, gain, alpha, w_query, w_key, w_value, w_out):
    saved_rows = saved_in[0]
    grad_rows = out_grad[0]
    gain_row = gain[0]
    query_weight = w_query[0]
    key_weight = w_key[0]
    value_weight = w_value[0]
    out_weight = w_out[0]
    all_saved, all_grads = (
        lax.all_gather(saved_rows, "tp", axis=0, tiled=True),
        lax.all_gather(grad_rows, "tp", axis=0, tiled=True),
    )
    query, keys, values = project_rows(all_saved, gain_row, query_weight, key_weight, value_weight)
    grad_heads = heads_back(all_grads, out_weight)
    grad_query, grad_keys, grad_values = attend_back(query, keys, values, grad_heads)
    rows = saved_rows.shape[0]
    total = jnp.zeros((lax.axis_size("tp") * rows, out_weight.shape[1]), jnp.float32)
    for grad_part, weight in (
        (grad_query, query_weight),
        (grad_keys, key_weight),
        (grad_values, value_weight),
    ):
        total = total + jnp.einsum(
            "te,de->td", grad_part, weight, preferred_element_type=jnp.float32
        )
    grad_normed = lax.psum_scatter(
        total.astype(jnp.bfloat16), "tp", scatter_dimension=0, tiled=True
    ).astype(jnp.float32)
    saved_float = saved_rows.astype(jnp.float32)
    factor = lax.rsqrt(jnp.mean(saved_float * saved_float, axis=-1, keepdims=True) + eps)
    scaled = grad_normed * gain_row
    inner = jnp.mean(scaled * saved_float, axis=-1, keepdims=True)
    grad_input = (
        grad_rows.astype(jnp.float32) + factor * (scaled - saved_float * factor * factor * inner)
    ).astype(jnp.bfloat16)
    updated = section_sums(alpha, grad_input, pending[0])
    return (grad_input[None], updated[None])


def solution(mesh):
    return jax.shard_map(
        on_device,
        mesh=mesh,
        in_specs=(
            P("section", "tp", None),
            P("section", "tp", None),
            P("section", "tp", None),
            P("section", None),
            P(),
            P("section", None, "tp"),
            P("section", None, "tp"),
            P("section", None, "tp"),
            P("section", "tp", None),
        ),
        out_specs=(P("section", "tp", None), P("section", "tp", None)),
        check_vma=False,
    )
```

time: 401 us -> 269 us (0.67)
  waiting for transfers between devices: 269 us -> 168 us
  Pallas kernels: 0 us -> 40.7 us
  other arithmetic: 43.7 us -> 6.85 us
  matrix products: 62.5 us -> 37.1 us
  local copies, waits for them, and re-layouts: 10.2 us -> 1.15 us
    all_gather x1 -> x0, waiting for transfers between devices: 95.2 us -> none  [on_device(): arrived = lax.all_gather(grad_input[None], 'section', axis=0, tiled=True)]
    pallas_call x0 -> x2, Pallas kernels: none -> 40.7 us  [the longest x1 32 us: section_sums(): pl.pallas_call(functools.partial(section_kernel, ny=4, nz=4), out_shape=j...]
    add x16 -> x0, other arithmetic: 29.1 us -> none  [add_one(): return total + coeffs[source] * arrived[source].astype(jnp.float32)]
    dynamic_slice x17 -> x0, local copies, waits for them, and re-layouts: 9.91 us -> none  [the longest x16 9.73 us: add_one(): return total + coeffs[source] * arrived[source].astype(jnp.float32)]
    sub x1 -> x0, matrix products: 8.15 us -> none  [attend_back(): weights = jnp.exp(scores - peak)]
    all_gather x1, waiting for transfers between devices: 43.5 us -> 35.8 us  [on_device(): lax.all_gather(grad_rows, 'tp', axis=0, tiled=True)]
    dot_general x5 -> x0, matrix products: 7.58 us -> none  [the longest x1 1.97 us: attend_back(): jnp.einsum('hqk,khe->hqe', probs, values, preferred_element_type=jnp.floa...]
    convert_element_type x2 -> x0, other arithmetic: 5.03 us -> none  [the longest x1 4.98 us: attend_back(): probs = weights.astype(jnp.bfloat16)]
  transfers between devices with their start and end apart: 4 -> 3, of which waited for: 4 -> 3; matrix products, arithmetic and copies ran while one was open for 1% -> 4% of each run, Pallas kernels for 0% -> 0%
where the time goes in v1:
time: 269 us; the launch traced here: 267 us
  waiting for transfers between devices  168 us (62%)
  Pallas kernels  40.7 us (15%)
  matrix products  37.1 us (14%)
  between operations  13.9 us (5%)
  other arithmetic  6.85 us (3%)
    reduce_scatter x1, waiting for transfers between devices, on_device(): lax.psum_scatter(total.astype(jnp.bfloat16), 'tp', scatter_dimension=0, t...  81.5 us
    all_gather x1, waiting for transfers between devices, on_device(): lax.all_gather(saved_rows, 'tp', axis=0, tiled=True)  49 us
    all_gather x1, waiting for transfers between devices, on_device(): lax.all_gather(grad_rows, 'tp', axis=0, tiled=True)  35.8 us
    pallas_call x1, Pallas kernels, section_sums(): pl.pallas_call(functools.partial(section_kernel, ny=4, nz=4), out_shape=j...  32 us
    dot_general x3, matrix products, on_device(): jnp.einsum('te,de->td', grad_part, weight, preferred_element_type=jnp.flo...  24.9 us
    pallas_call x1, Pallas kernels, attend_back(): pl.pallas_call(functools.partial(attend_kernel, block=256), out_shape=(ou...  8.67 us
  transfers between devices with their start and end apart: 3, of which 3 were waited for; matrix products, arithmetic and copies ran while one was open for 4% of the time, Pallas kernels for 0%

profile of v1, /device:TPU:8, one launch (start us, length us, event | category | flops | bytes accessed | tf_op | source)
XLA Modules:
  0.0 267.5 jit_solution(10570964260426785185)
XLA Ops:
  7.2 0.0 copy-start
  7.2 0.0 all-gather.5.cloned.1.call-start
  7.2 0.7 all-gather.5.cloned.1.call-update
  7.9 0.0 all-gather.7.cloned.1.call-start
  8.0 0.7 all-gather.7.cloned.1.call-update
  8.7 0.0 reduce-scatter.2.cloned.1.call-start
  8.7 49.0 %all-gather.5.cloned.1.call-done = bf16[1,1024,3072]{2,1,0:T(8,128)(2,1)} async-done(((bf16[1,64,3072]{2,1,0:T(8,128)(2,1)}), bf16[1,1024,3072]{2,1,0:T(8,128)(2,1)}) %all-gather.5.cloned.1.call-update) | async-done | bytes 6291472 | tf_op jit(solution)/shard_map/all_gather | solution.py:268
  57.7 4.2 %fusion = f32[1024]{0:T(1024)S(1)} fusion(bf16[1,1024,3072]{2,1,0:T(8,128)(2,1)} %all-gather.5.cloned.1.call-done), kind=kLoop, calls=%fused_computation.2 | loop fusion | flops 9436160 | bytes 6295552 | tf_op jit(solution)/shard_map/reduce_sum | solution.py:19
  62.0 0.3 copy-done.4
  62.3 3.4 %fusion.20.k_ref = bf16[1024,256]{1,0:T(8,128)(2,1)S(1)} fusion(bf16[1,3072,256]{2,1,0:T(8,128)(2,1)} %param.15, bf16[1,1024,3072]{2,1,0:T(8,128)(2,1)S(1)} %copy-done.4, f32[3072]{0:T(1024)S(1)} %bitcast.56, f32[1024]{0:T(1024)S(1)} %add_rsqrt_fusion), kind=kOutput, calls=%fused_computation.21 | convolution fusion | flops 1623457792 | bytes 8404992 | tf_op jit(solution)/shard_map/dot_general | solution.py:26
  65.7 0.0 copy-done.6
  65.7 1.9 fusion.23.v_ref
  67.6 1.9 fusion.17.q_ref
  69.5 35.8 %all-gather.7.cloned.1.call-done = bf16[1,1024,3072]{2,1,0:T(8,128)(2,1)} async-done(((bf16[1,64,3072]{2,1,0:T(8,128)(2,1)}), bf16[1,1024,3072]{2,1,0:T(8,128)(2,1)}) %all-gather.7.cloned.1.call-update) | async-done | bytes 6291472 | tf_op jit(solution)/shard_map/all_gather | solution.py:269
  105.3 5.0 %fusion.26.g_ref = bf16[1024,256]{1,0:T(8,128)(2,1)S(1)} fusion(bf16[1,256,3072]{2,1,0:T(8,128)(2,1)} %param.17, bf16[1,1024,3072]{2,1,0:T(8,128)(2,1)} %all-gather.7.cloned.1.call-done), kind=kOutput, calls=%fused_computation.23 | convolution fusion | flops 1610874880 | bytes 8388608 | tf_op jit(solution)/shard_map/td,ed->te/dot_general | solution.py:32
  110.3 8.7 %shard_map.104 = (bf16[1024,256]{1,0:T(8,128)(2,1)S(1)}, bf16[1024,256]{1,0:T(8,128)(2,1)S(1)}, bf16[1024,256]{1,0:T(8,128)(2,1)S(1)}) custom-call(bf16[1024,256]{1,0:T(8,128)(2,1)S(1)} %fusion.17.q_ref, bf16[1024,256]{1,0:T(8,128)(2,1)S(1)} %fusion.20.k_ref, bf16[1024,256]{1,0:T(8,128)(2,1)S(1)} %fusion.23.v_ref, bf16[1024,256]{1,0:T(8,128)(2,1)S(1)} %fusion.26.g_ref), custom_call_target="tpu_custom_call" | custom-call | flops 2000000000 | bytes 4000000 | tf_op jit(solution)/shard_map/pallas_call | solution.py:84
  119.0 0.0 copy-start.8
  119.0 6.4 %fusion.13 = f32[1024,3072]{1,0:T(8,128)} fusion(bf16[1024,256]{1,0:T(8,128)(2,1)S(1)} %get-tuple-element.5, bf16[1,3072,256]{2,1,0:T(8,128)(2,1)S(1)} %copy-done), kind=kOutput, calls=%fused_computation.16 | convolution fusion | flops 1610612736 | bytes 14680064 | tf_op jit(solution)/shard_map/te,de->td/dot_general | solution.py:281
  125.4 6.3 %fusion.9 = f32[1024,3072]{1,0:T(8,128)} fusion(bf16[1024,256]{1,0:T(8,128)(2,1)S(1)} %get-tuple-element.6, bf16[1,3072,256]{2,1,0:T(8,128)(2,1)S(1)} %copy-done.8), kind=kOutput, calls=%fused_computation.12 | convolution fusion | flops 1610612736 | bytes 14680064 | tf_op jit(solution)/shard_map/te,de->td/dot_general | solution.py:281
  131.7 12.2 %add_convert_fusion = bf16[1024,3072]{1,0:T(8,128)(2,1)} fusion(f32[1024,3072]{1,0:T(8,128)} %fusion.13, f32[1024,3072]{1,0:T(8,128)} %fusion.9, bf16[1024,256]{1,0:T(8,128)(2,1)S(1)} %get-tuple-element.7, bf16[1,3072,256]{2,1,0:T(8,128)(2,1)S(1)} %copy-done.7), kind=kOutput, calls=%fused_computation.5 | convolution fusion | flops 1620049920 | bytes 33554432 | tf_op jit(solution)/shard_map/te,de->td/dot_general | solution.py:281
  143.9 0.0 copy-start.3
  144.0 0.0 reduce-scatter.2.cloned.1.call-update
  144.0 81.5 %reduce-scatter.2.cloned.1.call-done = bf16[64,3072]{1,0:T(8,128)(2,1)} async-done(((bf16[1024,3072]{1,0:T(8,128)(2,1)}), bf16[64,3072]{1,0:T(8,128)(2,1)}) %reduce-scatter.2.cloned.1.call-update) | async-done | bytes 393232 | tf_op jit(solution)/shard_map/reduce_scatter | solution.py:284
  225.5 0.0 copy-done.5
  225.5 1.3 fusion.31
  226.8 0.0 copy-done.9
  226.8 1.3 fusion.37.mine_ref
  228.1 0.0 copy-start.1
  228.1 0.0 copy-done.2
  228.1 0.0 copy-done.3
  228.1 32.0 %shard_map.105 = bf16[64,3072]{1,0:T(8,128)(2,1)S(1)} custom-call(f32[16,16]{1,0:T(8,128)S(1)} %copy-done.3, bf16[64,3072]{1,0:T(8,128)(2,1)S(1)} %fusion.37.mine_ref, bf16[64,3072]{1,0:T(8,128)(2,1)S(1)} %bitcast.55), custom_call_target="tpu_custom_call" | custom-call | flops 10000000 | bytes 1000000 | tf_op jit(solution)/shard_map/pallas_call | solution.py:239
  260.2 0.7 copy.12
  (14 shorter events, 0.0 us)
Async XLA Ops:
  7.2 60.5 %copy-start = (bf16[1,3072,256]{2,1,0:T(8,128)(2,1)S(1)}, bf16[1,3072,256]{2,1,0:T(8,128)(2,1)}, u32[]{:S(2)}) copy-start(bf16[1,3072,256]{2,1,0:T(8,128)(2,1)} %param.14) | copy-start | bytes 4718596
  7.2 54.8 %copy-start.10 = (f32[1,3072]{1,0:T(1,128)S(1)}, f32[1,3072]{1,0:T(1,128)}, u32[]{:S(2)}) copy-start(f32[1,3072]{1,0:T(1,128)} %param.12) | copy-start | bytes 36868
  7.2 50.5 %all-gather.5.cloned.1.call-start = ((), (), s32[]{:S(2)}) async-start(), calls=%async_computation.2 | async-start | bytes 6684672 | tf_op jit(solution)/shard_map/all_gather | solution.py:268
  7.9 97.4 %all-gather.7.cloned.1.call-start = ((), (), s32[]{:S(2)}) async-start(), calls=%async_computation.3 | async-start | bytes 6684672 | tf_op jit(solution)/shard_map/all_gather | solution.py:269
  8.7 216.8 %reduce-scatter.2.cloned.1.call-start = ((), (), s32[]{:S(2)}) async-start(), calls=%async_computation.1 | async-start | bytes 6684672 | tf_op jit(solution)/shard_map/reduce_scatter | solution.py:284
  57.7 4.6 %copy-start.4 = (bf16[1,1024,3072]{2,1,0:T(8,128)(2,1)S(1)}, bf16[1,1024,3072]{2,1,0:T(8,128)(2,1)}, u32[]{:S(2)}) copy-start(bf16[1,1024,3072]{2,1,0:T(8,128)(2,1)} %all-gather.5.cloned.1.call-done) | copy-start | bytes 18874372
  62.3 3.4 %copy-start.6 = (bf16[1,3072,256]{2,1,0:T(8,128)(2,1)S(1)}, bf16[1,3072,256]{2,1,0:T(8,128)(2,1)}, u32[]{:S(2)}) copy-start(bf16[1,3072,256]{2,1,0:T(8,128)(2,1)} %param.16) | copy-start | bytes 4718596
  119.0 6.4 %copy-start.8 = (bf16[1,3072,256]{2,1,0:T(8,128)(2,1)S(1)}, bf16[1,3072,256]{2,1,0:T(8,128)(2,1)}, u32[]{:S(2)}) copy-start(bf16[1,3072,256]{2,1,0:T(8,128)(2,1)} %param.15) | copy-start | bytes 4718596
  125.4 6.3 %copy-start.7 = (bf16[1,3072,256]{2,1,0:T(8,128)(2,1)S(1)}, bf16[1,3072,256]{2,1,0:T(8,128)(2,1)}, u32[]{:S(2)}) copy-start(bf16[1,3072,256]{2,1,0:T(8,128)(2,1)} %param.16) | copy-start | bytes 4718596
  143.9 81.5 %copy-start.5 = (bf16[1,64,3072]{2,1,0:T(8,128)(2,1)S(1)}, bf16[1,64,3072]{2,1,0:T(8,128)(2,1)}, u32[]{:S(2)}) copy-start(bf16[1,64,3072]{2,1,0:T(8,128)(2,1)} %param.9) | copy-start | bytes 1179652
  143.9 82.8 %copy-start.9 = (bf16[1,64,3072]{2,1,0:T(8,128)(2,1)S(1)}, bf16[1,64,3072]{2,1,0:T(8,128)(2,1)}, u32[]{:S(2)}) copy-start(bf16[1,64,3072]{2,1,0:T(8,128)(2,1)} %param.10) | copy-start | bytes 1179652
  143.9 84.2 %copy-start.2 = (bf16[1,64,3072]{2,1,0:T(8,128)(2,1)S(1)}, bf16[1,64,3072]{2,1,0:T(8,128)(2,1)}, u32[]{:S(2)}) copy-start(bf16[1,64,3072]{2,1,0:T(8,128)(2,1)} %param.11) | copy-start | bytes 1179652
  143.9 84.2 %copy-start.3 = (f32[16,16]{1,0:T(8,128)S(1)}, f32[16,16]{1,0:T(8,128)}, u32[]{:S(2)}) copy-start(f32[16,16]{1,0:T(8,128)} %alpha_ref.1) | copy-start | bytes 3076
  228.1 32.8 %copy-start.1 = (bf16[64,3072]{1,0:T(8,128)(2,1)}, bf16[64,3072]{1,0:T(8,128)(2,1)S(1)}, u32[]{:S(2)}) copy-start(bf16[64,3072]{1,0:T(8,128)(2,1)S(1)} %fusion.37.mine_ref) | copy-start | bytes 1179652
Sparse Core Ops, SparseCore 0:
  9.9 47.7 all-gather.4
  59.6 45.6 all-gather.6
  144.1 81.3 reduce-scatter.1

commit v2 on v1

--- a/solution.py
+++ b/solution.py
@@ -14,33 +14,19 @@
 eps = 1e-05
 
 
-def normalize(rows, gain_row):
-    values = rows.astype(jnp.float32)
-    factor = lax.rsqrt(jnp.mean(values * values, axis=-1, keepdims=True) + eps)
-    return (values * factor * gain_row).astype(jnp.bfloat16)
-
-
-def project_rows(rows, gain_row, query_weight, key_weight, value_weight):
-    normed = normalize(rows, gain_row)
-    query = jnp.dot(normed, query_weight, preferred_element_type=jnp.float32).astype(jnp.bfloat16)
-    keys = jnp.dot(normed, key_weight, preferred_element_type=jnp.float32).astype(jnp.bfloat16)
-    values = jnp.dot(normed, value_weight, preferred_element_type=jnp.float32).astype(jnp.bfloat16)
-    return query, keys, values
-
-
-def heads_back(grad_rows, out_weight):
-    product = jnp.einsum("td,ed->te", grad_rows, out_weight, preferred_element_type=jnp.float32)
-    return product.astype(jnp.bfloat16)
-
-
 def dot(a, b, ca, cb):
     return lax.dot_general(a, b, (((ca,), (cb,)), ((), ())), preferred_element_type=jnp.float32)
 
 
-def attend_kernel(q_ref, k_ref, v_ref, g_ref, dq_ref, dk_ref, dv_ref, dk_acc, dv_acc, *, block):
+def attend_kernel(in_ref, out_ref, q_ref, k_ref, v_ref, g_ref, dk_acc, dv_acc, *, block, rows):
     tokens, width = q_ref.shape
     scale = 1.0 / math.sqrt(HEAD)
     log2e = math.log2(math.e)
+    places = [(chip, core, pl.ds((2 * chip + core) * rows, rows))
+              for chip in range(tokens // (2 * rows)) for core in (0, 1)]
+    for j, ref in enumerate((q_ref, k_ref, v_ref, g_ref)):
+        for chip, core, here in places:
+            ref[here, :] = in_ref[core, j, pl.ds(chip * rows, rows), :]
     below = lax.broadcasted_iota(jnp.int32, (block, block), 0) <= lax.broadcasted_iota(
         jnp.int32, (block, block), 1
     )
@@ -50,8 +36,8 @@
         values_t = v_ref[:, cols].T
         for step in reversed(range(tokens // block)):
             n = (step + 1) * block
-            rows = pl.ds(step * block, block)
-            query, grad = q_ref[rows, cols], g_ref[rows, cols]
+            mine = pl.ds(step * block, block)
+            query, grad = q_ref[mine, cols], g_ref[mine, cols]
             scores = dot(k_ref[pl.ds(0, n), cols], query, 1, 1) * (scale * log2e)
             last = jnp.where(below, scores[n - block :], -1e30)
             scores = last if step == 0 else jnp.concatenate((scores[: n - block], last), axis=0)
@@ -64,7 +50,11 @@
             delta = jnp.sum(grad_t * output_t, axis=0, keepdims=True)
             grad_probs = dot(v_ref[pl.ds(0, n), cols], grad, 1, 1)
             grad_scores = (weights * ((grad_probs - delta) * scale)).astype(jnp.bfloat16)
-            dq_ref[rows, cols] = dot(keys_t[:, :n], grad_scores, 1, 0).T.astype(jnp.bfloat16)
+            grad_query = dot(keys_t[:, :n], grad_scores, 1, 0).T.astype(jnp.bfloat16)
+            for chip, core, here in places:
+                offset = (2 * chip + core) * rows - step * block
+                if 0 <= offset < block:
+                    out_ref[core, 0, pl.ds(chip * rows, rows), cols] = grad_query[offset : offset + rows]
             more_k = dot(grad_scores, query, 1, 0)
             more_v = dot(probs, grad, 1, 0)
             if step == tokens // block - 1:
@@ -73,23 +63,416 @@
             else:
                 dk_acc[pl.ds(0, n)] += more_k
                 dv_acc[pl.ds(0, n)] += more_v
-        dk_ref[:, cols] = dk_acc[...].astype(jnp.bfloat16)
-        dv_ref[:, cols] = dv_acc[...].astype(jnp.bfloat16)
-
-
-def attend_back(query, keys, values, grad_heads):
-    tokens, width = query.shape
-    out = jax.ShapeDtypeStruct((tokens, width), jnp.bfloat16)
+        for j, acc in ((1, dk_acc), (2, dv_acc)):
+            for chip, core, here in places:
+                out_ref[core, j, pl.ds(chip * rows, rows), cols] = acc[here, :].astype(jnp.bfloat16)
+
+
+def attend_back(heads, rows):
+    _, _, half, width = heads.shape
+    tokens = 2 * half
     whole = pl.BlockSpec(memory_space=pltpu.VMEM)
     return pl.pallas_call(
-        functools.partial(attend_kernel, block=256),
-        out_shape=(out, out, out),
-        in_specs=[whole] * 4,
-        out_specs=(whole,) * 3,
-        scratch_shapes=[pltpu.VMEM((tokens, HEAD), jnp.float32)] * 2,
+        functools.partial(attend_kernel, block=256, rows=rows),
+        out_shape=jax.ShapeDtypeStruct((2, 3, half, width), jnp.bfloat16),
+        in_specs=[whole],
+        out_specs=whole,
+        scratch_shapes=[pltpu.VMEM((tokens, width), jnp.bfloat16)] * 4
+        + [pltpu.VMEM((tokens, HEAD), jnp.float32)] * 2,
         compiler_params=pltpu.CompilerParams(vmem_limit_bytes=40 * 2**20),
         cost_estimate=pl.CostEstimate(flops=2 * 10**9, bytes_accessed=4 * 10**6, transcendentals=10**6),
-    )(query, keys, values, grad_heads)
+    )(heads)
+
+
+def tile_loop(rows, depth, wide, body):
+    tall = rows // 16
+
+    def step(i, carry):
+        rr = pl.multiple_of(lax.rem(i, tall) * 16, 16)
+        cc = pl.multiple_of((i // tall) * wide, wide)
+        body(pl.ds(rr, 16), pl.ds(cc, wide))
+        return carry
+
+    lax.fori_loop(0, tall * (depth // wide), step, 0)
+
+
+def greet(others):
+    barrier = pltpu.get_barrier_semaphore()
+    for other in others:
+        pl.semaphore_signal(barrier, inc=1, device_id={"tp": other}, device_id_type=MESH)
+    pl.semaphore_wait(barrier, len(others))
+
+
+def neighbours():
+    place = lax.axis_index("tp")
+    x, z, core = place // 4, lax.rem(place // 2, 2), lax.rem(place, 2)
+    right = lax.rem(x + 1, 4) * 4 + z * 2 + core
+    left = lax.rem(x + 3, 4) * 4 + z * 2 + core
+    across = x * 4 + (1 - z) * 2 + core
+    twin = x * 4 + z * 2 + (1 - core)
+    return x, z, core, right, left, across, twin
+
+
+def project_kernel(saved_ref, grad_ref, gain_ref, wq_ref, wk_ref, wv_ref, wo_ref, heads_ref, twin_ref,
+                   normed, grads, weights, out_weights, theirs, send_sem, recv_sem, load_sem, store_sem):
+    x, z, core, right, left, across, twin = neighbours()
+    rows, depth = saved_ref.shape
+    width = wq_ref.shape[1]
+    pair = 2 * rows
+    half = rows // 2
+    lo, hi = pl.ds(0, half), pl.ds(half, half)
+    other = 1 - z
+    sends = []
+
+    loads = [
+        pltpu.make_async_copy(wq_ref, weights.at[0, 0], load_sem.at[0]),
+        pltpu.make_async_copy(wk_ref, weights.at[0, 1], load_sem.at[1]),
+        pltpu.make_async_copy(wv_ref, weights.at[0, 2], load_sem.at[2]),
+        pltpu.make_async_copy(wo_ref, out_weights.at[0], load_sem.at[3]),
+    ]
+    greet((right, left, across, twin))
+
+    def go(index, src, dst, to):
+        c = pltpu.make_async_remote_copy(
+            src_ref=src, dst_ref=dst, send_sem=send_sem.at[index], recv_sem=recv_sem.at[index],
+            device_id={"tp": to}, device_id_type=MESH,
+        )
+        c.start()
+        sends.append(c)
+        return c
+
+    g_right = go(0, grad_ref, grads.at[1, z], right)
+    g_left = go(1, grad_ref, grads.at[3, z], left)
+
+    def norm(i, carry):
+        here = pl.ds(pl.multiple_of(i * 16, 16), 16)
+        values = saved_ref[here, :].astype(jnp.float32)
+        factor = lax.rsqrt(jnp.mean(values * values, axis=-1, keepdims=True) + eps)
+        normed[0, z, here, :] = (values * factor * gain_ref[...]).astype(jnp.bfloat16)
+        return carry
+
+    lax.fori_loop(0, rows // 16, norm, 0)
+    n_across = go(8, normed.at[0, z], normed.at[0, z], across)
+    n_right = go(9, normed.at[0, z], normed.at[1, z], right)
+    n_left = go(10, normed.at[0, z], normed.at[3, z], left)
+    g_across = go(4, grad_ref, grads.at[0, z], across)
+    for c in loads:
+        c.start()
+    w_twin = [
+        go(17, wq_ref, weights.at[1, 0], twin),
+        go(18, wk_ref, weights.at[1, 1], twin),
+        go(19, wv_ref, weights.at[1, 2], twin),
+        go(20, wo_ref, out_weights.at[1], twin),
+    ]
+    grads[0, z] = grad_ref[...]
+
+    def place_of(r):
+        return pl.ds(pl.multiple_of(lax.rem(x + 4 - r, 4) * pair, pair), pair)
+
+    def project(r, which):
+        here = place_of(r)
+
+        def one(j, carry):
+            block = normed[r].reshape(pair, depth)
+            result = dot(block, weights[which, j], 1, 0).astype(jnp.bfloat16)
+            if which == 0:
+                heads_ref[core, j, here, :] = result
+            else:
+                theirs[j, here, :] = result
+            return carry
+
+        lax.fori_loop(0, 3, one, 0)
+
+    def project_grads(r, which):
+        here = place_of(r)
+        result = dot(grads[r].reshape(pair, depth), out_weights[which], 1, 1).astype(jnp.bfloat16)
+        if which == 0:
+            heads_ref[core, 3, here, :] = result
+        else:
+            theirs[3, here, :] = result
+
+    results = []
+
+    def hand_over(index, r, first, count):
+        js, here = pl.ds(first, count), place_of(r)
+        results.append(go(index, theirs.at[js, here], heads_ref.at[core, js, here], twin))
+
+    n_across.wait_recv()
+    no_right = go(11, normed.at[0, other], normed.at[1, other], right)
+    no_left = go(12, normed.at[0, other], normed.at[3, other], left)
+    for c in loads[:3]:
+        c.wait()
+    project(0, 0)
+    g_right.wait_recv()
+    g_relay_right = go(2, grads.at[1, z, lo], grads.at[2, z, lo], right)
+    g_one = go(5, grads.at[1, z], grads.at[1, z], across)
+    g_left.wait_recv()
+    g_relay_left = go(3, grads.at[3, z, hi], grads.at[2, z, hi], left)
+    g_three = go(6, grads.at[3, z], grads.at[3, z], across)
+    loads[3].wait()
+    n_right.wait_recv()
+    n_relay_right = go(13, normed.at[1, z, lo], normed.at[2, z, lo], right)
+    n_left.wait_recv()
+    n_relay_left = go(14, normed.at[3, z, hi], normed.at[2, z, hi], left)
+    g_relay_right.wait_recv()
+    g_relay_left.wait_recv()
+    g_two = go(7, grads.at[2, z], grads.at[2, z], across)
+    g_across.wait_recv()
+    project_grads(0, 0)
+    no_right.wait_recv()
+    no_relay_right = go(15, normed.at[1, other, lo], normed.at[2, other, lo], right)
+    no_left.wait_recv()
+    no_relay_left = go(16, normed.at[3, other, hi], normed.at[2, other, hi], left)
+    project(1, 0)
+    project(3, 0)
+    for c in w_twin:
+        c.wait_recv()
+    stores = [
+        pltpu.make_async_copy(weights.at[1, j], twin_ref.at[j], store_sem.at[j]) for j in range(3)
+    ]
+    for c in stores:
+        c.start()
+    for index, r in ((21, 0), (22, 1), (23, 3)):
+        project(r, 1)
+        hand_over(index, r, 0, 3)
+    project_grads(0, 1)
+    hand_over(25, 0, 3, 1)
+    for index, r, c in ((26, 1, g_one), (27, 3, g_three)):
+        c.wait_recv()
+        project_grads(r, 1)
+        hand_over(index, r, 3, 1)
+        project_grads(r, 0)
+    for c in (n_relay_right, n_relay_left, no_relay_right, no_relay_left):
+        c.wait_recv()
+    project(2, 1)
+    hand_over(24, 2, 0, 3)
+    project(2, 0)
+    g_two.wait_recv()
+    project_grads(2, 1)
+    hand_over(28, 2, 3, 1)
+    project_grads(2, 0)
+    for c in results:
+        c.wait_recv()
+    for c in sends:
+        c.wait_send()
+    for c in stores:
+        c.wait()
+
+
+def project_all(saved, grad, gain, wq, wk, wv, wo):
+    rows, depth = saved.shape
+    width = wq.shape[1]
+    vmem = pl.BlockSpec(memory_space=pltpu.VMEM)
+    hbm = pl.BlockSpec(memory_space=pl.ANY)
+    return pl.pallas_call(
+        project_kernel,
+        out_shape=(
+            jax.ShapeDtypeStruct((2, 4, 8 * rows, width), jnp.bfloat16),
+            jax.ShapeDtypeStruct((3, depth, width), jnp.bfloat16),
+        ),
+        in_specs=[vmem, vmem, vmem, hbm, hbm, hbm, hbm],
+        out_specs=(vmem, hbm),
+        scratch_shapes=[
+            pltpu.VMEM((4, 2, rows, depth), jnp.bfloat16),
+            pltpu.VMEM((4, 2, rows, depth), jnp.bfloat16),
+            pltpu.VMEM((2, 3, depth, width), jnp.bfloat16),
+            pltpu.VMEM((2, width, depth), jnp.bfloat16),
+            pltpu.VMEM((4, 8 * rows, width), jnp.bfloat16),
+            pltpu.SemaphoreType.DMA((29,)),
+            pltpu.SemaphoreType.DMA((29,)),
+            pltpu.SemaphoreType.DMA((4,)),
+            pltpu.SemaphoreType.DMA((3,)),
+        ],
+        compiler_params=pltpu.CompilerParams(
+            collective_id=1, has_side_effects=True, vmem_limit_bytes=56 * 2**20
+        ),
+        cost_estimate=pl.CostEstimate(flops=6 * 10**9, bytes_accessed=10**7, transcendentals=0),
+    )(saved, grad, gain, wq, wk, wv, wo)
+
+
+def input_kernel(d_ref, wq_ref, wk_ref, wv_ref, twin_ref, saved_ref, grad_ref, gain_ref, out_ref,
+                 weights, theirs, part, za, xa1, xa2, xb1, xb2, zb, summed, send_sem, recv_sem, load_sem):
+    x, z, core, right, left, across, twin = neighbours()
+    rows, depth = saved_ref.shape
+    wide = part.shape[4]
+    pair = 2 * rows
+    lo, hi = pl.ds(0, rows // 2), pl.ds(rows // 2, rows // 2)
+    other = 1 - z
+    chunk = 512
+    chunks = depth // chunk
+    f32 = jnp.float32
+    sends = []
+
+    loads = []
+    for n in range(chunks):
+        here = pl.ds(n * chunk, chunk)
+        sources = [w.at[here] for w in (wq_ref, wk_ref, wv_ref)] + [twin_ref.at[j, here] for j in range(3)]
+        loads.append([
+            pltpu.make_async_copy(s, weights.at[j, here], load_sem.at[n, j]) for j, s in enumerate(sources)
+        ])
+    for n in range(chunks):
+        for c in loads[n]:
+            c.start()
+    greet((right, left, across, twin))
+
+    def go(index, src, dst, to):
+        c = pltpu.make_async_remote_copy(
+            src_ref=src, dst_ref=dst, send_sem=send_sem.at[index], recv_sem=recv_sem.at[index],
+            device_id={"tp": to}, device_id_type=MESH,
+        )
+        c.start()
+        sends.append(c)
+        return c
+
+    swap = go(0, d_ref.at[1 - core], theirs, twin)
+
+    def one_chunk(r, n):
+        here = pl.ds(pl.multiple_of(lax.rem(x + r, 4) * pair, pair), pair)
+        cols = pl.ds(pl.multiple_of(n * chunk, chunk), chunk)
+        total = dot(d_ref[core, 0, here, :], weights[0, cols, :], 1, 1)
+        for j in (1, 2):
+            total += dot(d_ref[core, j, here, :], weights[j, cols, :], 1, 1)
+        for j in (0, 1, 2):
+            total += dot(theirs[j, here, :], weights[3 + j, cols, :], 1, 1)
+        per = wide // chunk
+        into = pl.ds(pl.multiple_of(lax.rem(n, per) * chunk, chunk), chunk)
+        part[r, :, n // per, :, into] = total.astype(jnp.bfloat16).reshape(2, rows, chunk)
+
+    def block(r):
+        def step(n, carry):
+            one_chunk(r, n)
+            return carry
+
+        lax.fori_loop(0, chunks, step, 0)
+
+    def add(target, source, count):
+        def body(here, cols):
+            target[here, cols] = (
+                target[here, cols].astype(f32) + source[here, cols].astype(f32)
+            ).astype(jnp.bfloat16)
+
+        tile_loop(count, wide, chunk, body)
+
+    swap.wait_recv()
+    for n in range(chunks):
+        for c in loads[n]:
+            c.wait()
+        one_chunk(2, n)
+    xb1_right = go(1, part.at[2, 0, 1], xb1.at[0], right)
+    xb1_left = go(2, part.at[2, 1, 1], xb1.at[1], left)
+    za_two = go(3, part.at[2, other, 0], za.at[2], across)
+    block(1)
+    xb2_right = [None, go(4, part.at[1, 1, 1], xb2.at[0, 1], right)]
+    za_one = go(5, part.at[1, other, 0], za.at[1], across)
+    block(3)
+    xb2_left = [go(6, part.at[3, 0, 1], xb2.at[1, 0], left), None]
+    za_three = go(7, part.at[3, other, 0], za.at[3], across)
+    xb1_right.wait_recv()
+    add(part.at[1, 0, 1], xb1.at[0], rows)
+    xb2_right[0] = go(8, part.at[1, 0, 1], xb2.at[0, 0], right)
+    xb1_left.wait_recv()
+    add(part.at[3, 1, 1], xb1.at[1], rows)
+    xb2_left[1] = go(9, part.at[3, 1, 1], xb2.at[1, 1], left)
+    za_two.wait_recv()
+    add(part.at[2, z, 0], za.at[2], rows)
+    xa1_right = go(10, part.at[2, z, 0, lo], xa1.at[lo], right)
+    xa1_left = go(11, part.at[2, z, 0, hi], xa1.at[hi], left)
+    block(0)
+    za_zero = go(12, part.at[0, other, 0], za.at[0], across)
+    za_one.wait_recv()
+    add(part.at[1, z, 0], za.at[1], rows)
+    xa1_right.wait_recv()
+    add(part.at[1, z, 0, lo], xa1.at[lo], rows // 2)
+    xa2_right = go(13, part.at[1, z, 0], xa2.at[0], right)
+    za_three.wait_recv()
+    add(part.at[3, z, 0], za.at[3], rows)
+    xa1_left.wait_recv()
+    add(part.at[3, z, 0, hi], xa1.at[hi], rows // 2)
+    xa2_left = go(14, part.at[3, z, 0], xa2.at[1], left)
+    for c in xb2_right + xb2_left:
+        c.wait_recv()
+
+    def fold(here, cols):
+        total = part[0, other, 1, here, cols].astype(f32) + xb2[0, other, here, cols].astype(f32)
+        part[0, other, 1, here, cols] = (total + xb2[1, other, here, cols].astype(f32)).astype(jnp.bfloat16)
+
+    tile_loop(rows, wide, chunk, fold)
+    zb_across = go(15, part.at[0, other, 1], zb, across)
+
+    def fold_own(here, cols):
+        total = part[0, z, 1, here, cols].astype(f32) + xb2[0, z, here, cols].astype(f32)
+        summed[1, here, cols] = total + xb2[1, z, here, cols].astype(f32)
+
+    tile_loop(rows, wide, chunk, fold_own)
+    za_zero.wait_recv()
+    xa2_right.wait_recv()
+    xa2_left.wait_recv()
+
+    def fold_first(here, cols):
+        total = part[0, z, 0, here, cols].astype(f32) + za[0, here, cols].astype(f32)
+        total = total + xa2[0, here, cols].astype(f32)
+        summed[0, here, cols] = total + xa2[1, here, cols].astype(f32)
+
+    tile_loop(rows, wide, chunk, fold_first)
+    zb_across.wait_recv()
+
+    def norm_back(i, carry):
+        here = pl.ds(pl.multiple_of(i * 16, 16), 16)
+        values = saved_ref[here, :].astype(f32)
+        factor = lax.rsqrt(jnp.mean(values * values, axis=-1, keepdims=True) + eps)
+        inner = jnp.zeros((16, 1), f32)
+        for h in (0, 1):
+            cols = pl.ds(h * wide, wide)
+            scaled = summed[h, here, :]
+            if h == 1:
+                scaled = scaled + zb[here, :].astype(f32)
+            scaled = scaled * gain_ref[:, cols]
+            summed[h, here, :] = scaled
+            inner = inner + jnp.sum(scaled * saved_ref[here, cols].astype(f32), axis=-1, keepdims=True)
+        inner = inner * (1.0 / depth) * factor * factor
+        for h in (0, 1):
+            cols = pl.ds(h * wide, wide)
+            term = summed[h, here, :] - saved_ref[here, cols].astype(f32) * inner
+            out_ref[here, cols] = (grad_ref[here, cols].astype(f32) + factor * term).astype(jnp.bfloat16)
+        return carry
+
+    lax.fori_loop(0, rows // 16, norm_back, 0)
+    for c in sends:
+        c.wait_send()
+
+
+def input_grads(d, wq, wk, wv, twin, saved, grad, gain):
+    rows, depth = saved.shape
+    width = wq.shape[1]
+    wide = depth // 2
+    vmem = pl.BlockSpec(memory_space=pltpu.VMEM)
+    hbm = pl.BlockSpec(memory_space=pl.ANY)
+    bf16 = jnp.bfloat16
+    return pl.pallas_call(
+        input_kernel,
+        out_shape=jax.ShapeDtypeStruct((rows, depth), bf16),
+        in_specs=[vmem, hbm, hbm, hbm, hbm, vmem, vmem, vmem],
+        out_specs=vmem,
+        scratch_shapes=[
+            pltpu.VMEM((6, depth, width), bf16),
+            pltpu.VMEM((3, 8 * rows, width), bf16),
+            pltpu.VMEM((4, 2, 2, rows, wide), bf16),
+            pltpu.VMEM((4, rows, wide), bf16),
+            pltpu.VMEM((rows, wide), bf16),
+            pltpu.VMEM((2, rows, wide), bf16),
+            pltpu.VMEM((2, rows, wide), bf16),
+            pltpu.VMEM((2, 2, rows, wide), bf16),
+            pltpu.VMEM((rows, wide), bf16),
+            pltpu.VMEM((2, rows, wide), jnp.float32),
+            pltpu.SemaphoreType.DMA((16,)),
+            pltpu.SemaphoreType.DMA((16,)),
+            pltpu.SemaphoreType.DMA((depth // 512, 6)),
+        ],
+        compiler_params=pltpu.CompilerParams(
+            collective_id=2, has_side_effects=True, vmem_limit_bytes=56 * 2**20
+        ),
+        cost_estimate=pl.CostEstimate(flops=5 * 10**9, bytes_accessed=10**7, transcendentals=0),
+    )(d, wq, wk, wv, twin, saved, grad, gain)
 
 
 def section_kernel(alpha_ref, mine_ref, pending_ref, out_ref, gather, part, stage, arrived,
@@ -257,40 +640,11 @@
 
 
 def on_device(saved_in, out_grad, pending, gain, alpha, w_query, w_key, w_value, w_out):
-    saved_rows = saved_in[0]
-    grad_rows = out_grad[0]
-    gain_row = gain[0]
-    query_weight = w_query[0]
-    key_weight = w_key[0]
-    value_weight = w_value[0]
-    out_weight = w_out[0]
-    all_saved, all_grads = (
-        lax.all_gather(saved_rows, "tp", axis=0, tiled=True),
-        lax.all_gather(grad_rows, "tp", axis=0, tiled=True),
-    )
-    query, keys, values = project_rows(all_saved, gain_row, query_weight, key_weight, value_weight)
-    grad_heads = heads_back(all_grads, out_weight)
-    grad_query, grad_keys, grad_values = attend_back(query, keys, values, grad_heads)
-    rows = saved_rows.shape[0]
-    total = jnp.zeros((lax.axis_size("tp") * rows, out_weight.shape[1]), jnp.float32)
-    for grad_part, weight in (
-        (grad_query, query_weight),
-        (grad_keys, key_weight),
-        (grad_values, value_weight),
-    ):
-        total = total + jnp.einsum(
-            "te,de->td", grad_part, weight, preferred_element_type=jnp.float32
-        )
-    grad_normed = lax.psum_scatter(
-        total.astype(jnp.bfloat16), "tp", scatter_dimension=0, tiled=True
-    ).astype(jnp.float32)
-    saved_float = saved_rows.astype(jnp.float32)
-    factor = lax.rsqrt(jnp.mean(saved_float * saved_float, axis=-1, keepdims=True) + eps)
-    scaled = grad_normed * gain_row
-    inner = jnp.mean(scaled * saved_float, axis=-1, keepdims=True)
-    grad_input = (
-        grad_rows.astype(jnp.float32) + factor * (scaled - saved_float * factor * factor * inner)
-    ).astype(jnp.bfloat16)
+    saved, grad = saved_in[0], out_grad[0]
+    wq, wk, wv, wo = w_query[0], w_key[0], w_value[0], w_out[0]
+    heads, twin = project_all(saved, grad, gain, wq, wk, wv, wo)
+    back = attend_back(heads, saved.shape[0])
+    grad_input = input_grads(back, wq, wk, wv, twin, saved, grad, gain)
     updated = section_sums(alpha, grad_input, pending[0])
     return (grad_input[None], updated[None])
 

time: 269 us -> 145 us (0.54)
  waiting for transfers between devices: 168 us -> 0 us
  Pallas kernels: 40.7 us -> 136 us
  matrix products: 37.1 us -> 0 us
  between operations: 13.9 us -> 0.7 us
  other arithmetic: 6.85 us -> 0 us
  local copies, waits for them, and re-layouts: 1.15 us -> 5.23 us
    pallas_call x1 -> x3, Pallas kernels: 8.67 us -> 100 us  [the longest x1 54.5 us: project_all(): pl.pallas_call(project_kernel, out_shape=(jax.ShapeDtypeStruct((2, 4, 8 *...]
    all_gather x2 -> x0, waiting for transfers between devices: 84.8 us -> none  [the longest x1 49 us: on_device(): lax.all_gather(saved_rows, 'tp', axis=0, tiled=True)]
    reduce_scatter x1 -> x0, waiting for transfers between devices: 81.5 us -> none  [on_device(): lax.psum_scatter(total.astype(jnp.bfloat16), 'tp', scatter_dimension=0, t...]
    dot_general x7 -> x0, matrix products: 37.1 us -> none  [the longest x3 24.9 us: on_device(): jnp.einsum('te,de->td', grad_part, weight, preferred_element_type=jnp.flo...]
    reduce_sum x2 -> x0, other arithmetic: 5.52 us -> none  [the longest x1 4.23 us: normalize(): factor = lax.rsqrt(jnp.mean(values * values, axis=-1, keepdims=True) + eps)]
    unnamed x23 -> x12, local copies, waits for them, and re-layouts: 1.15 us -> 5.23 us
    pallas_call x1, Pallas kernels: 32 us -> 36 us  [section_sums(): pl.pallas_call(functools.partial(section_kernel, ny=4, nz=4), out_shape=j...]
  transfers between devices with their start and end apart: 3 -> 0, of which waited for: 3 -> 0; matrix products, arithmetic and copies ran while one was open for 4% -> 0% of each run, Pallas kernels for 0% -> 0%
where the time goes in v2:
time: 145 us; the launch traced here: 142 us
  Pallas kernels  136 us (94%)
  local copies, waits for them, and re-layouts  5.23 us (4%)
    pallas_call x1, Pallas kernels, project_all(): pl.pallas_call(project_kernel, out_shape=(jax.ShapeDtypeStruct((2, 4, 8 *...  54.5 us
    pallas_call x1, Pallas kernels, input_grads(): pl.pallas_call(input_kernel, out_shape=jax.ShapeDtypeStruct((rows, depth)...  37.2 us
    pallas_call x1, Pallas kernels, section_sums(): pl.pallas_call(functools.partial(section_kernel, ny=4, nz=4), out_shape=j...  36 us
    pallas_call x1, Pallas kernels, attend_back(): pl.pallas_call(functools.partial(attend_kernel, block=256, rows=rows), ou...  8.59 us
    unnamed x12, local copies, waits for them, and re-layouts  5.23 us

profile of v2, /device:TPU:8, one launch (start us, length us, event | category | flops | bytes accessed | tf_op | source)
XLA Modules:
  0.0 142.2 jit_solution(11119086079722958250)
XLA Ops:
  0.6 54.5 %shard_map.104 = (bf16[2,4,512,256]{3,2,1,0:T(8,128)(2,1)}, bf16[3,3072,256]{2,1,0:T(8,128)(2,1)}) custom-call(bf16[64,3072]{1,0:T(8,128)(2,1)} %bitcast.19, bf16[64,3072]{1,0:T(8,128)(2,1)} %bitcast.21, f32[1,3072]{1,0:T(1,128)} %gain_ref.3, bf16[3072,256]{1,0:T(8,128)(2,1)} %bitcast.13, bf16[3072,256]{1,0:T(8,128)(2,1)} %bitcast.15, ...), custom_call_target="tpu_custom_call" | custom-call | flops 6000000000 | bytes 10000000 | tf_op jit(solution)/shard_map/pallas_call | solution.py:267
  55.2 0.0 copy-start.3
  55.2 1.6 %copy-done.3 = bf16[2,4,512,256]{3,2,1,0:T(8,128)(2,1)S(1)} copy-done((bf16[2,4,512,256]{3,2,1,0:T(8,128)(2,1)S(1)}, bf16[2,4,512,256]{3,2,1,0:T(8,128)(2,1)}, u32[]{:S(2)}) %copy-start.3) | copy-done | bytes 2097176
  56.8 8.6 %shard_map.105.d_ref = bf16[2,3,512,256]{3,2,1,0:T(8,128)(2,1)S(1)} custom-call(bf16[2,4,512,256]{3,2,1,0:T(8,128)(2,1)S(1)} %copy-done.3), custom_call_target="tpu_custom_call" | custom-call | flops 2000000000 | bytes 4000000 | tf_op jit(solution)/shard_map/pallas_call | solution.py:75
  65.4 0.0 copy-start.4
  65.4 1.2 copy-done.4
  66.5 0.0 copy-start.1
  66.5 0.0 copy-start.2
  66.5 37.2 %shard_map.106.mine_ref = bf16[64,3072]{1,0:T(8,128)(2,1)} custom-call(bf16[2,3,512,256]{3,2,1,0:T(8,128)(2,1)} %copy-done.4, bf16[3072,256]{1,0:T(8,128)(2,1)} %bitcast.14, bf16[3072,256]{1,0:T(8,128)(2,1)} %bitcast.16, bf16[3072,256]{1,0:T(8,128)(2,1)} %bitcast.18, bf16[3,3072,256]{2,1,0:T(8,128)(2,1)} %get-tuple-element.5.twin_ref, ...), custom_call_target="tpu_custom_call" | custom-call | flops 5000000000 | bytes 10000000 | tf_op jit(solution)/shard_map/pallas_call | solution.py:451
  103.7 0.0 copy-done.1
  103.7 0.0 copy-done.2
  103.8 0.0 copy-start
  103.8 1.0 copy-done
  104.8 36.0 %shard_map.107 = bf16[64,3072]{1,0:T(8,128)(2,1)S(1)} custom-call(f32[16,16]{1,0:T(8,128)S(1)} %copy-done.2, bf16[64,3072]{1,0:T(8,128)(2,1)S(1)} %copy-done, bf16[64,3072]{1,0:T(8,128)(2,1)S(1)} %bitcast.11), custom_call_target="tpu_custom_call" | custom-call | flops 10000000 | bytes 1000000 | tf_op jit(solution)/shard_map/pallas_call | solution.py:622
  140.7 0.7 copy.13
  141.5 0.7 copy.14
Async XLA Ops:
  55.2 1.6 %copy-start.3 = (bf16[2,4,512,256]{3,2,1,0:T(8,128)(2,1)S(1)}, bf16[2,4,512,256]{3,2,1,0:T(8,128)(2,1)}, u32[]{:S(2)}) copy-start(bf16[2,4,512,256]{3,2,1,0:T(8,128)(2,1)} %get-tuple-element.4.in_ref) | copy-start | bytes 6291460
  65.4 1.2 copy-start.4
  66.5 37.2 %copy-start.1 = (bf16[1,64,3072]{2,1,0:T(8,128)(2,1)S(1)}, bf16[1,64,3072]{2,1,0:T(8,128)(2,1)}, u32[]{:S(2)}) copy-start(bf16[1,64,3072]{2,1,0:T(8,128)(2,1)} %param.11) | copy-start | bytes 1179652
  66.5 37.2 %copy-start.2 = (f32[16,16]{1,0:T(8,128)S(1)}, f32[16,16]{1,0:T(8,128)}, u32[]{:S(2)}) copy-start(f32[16,16]{1,0:T(8,128)} %alpha_ref.1) | copy-start | bytes 3076
  103.8 1.0 copy-start

commit v3 on v0

v3 whole, which is shorter than its diff:
```python
import math

import jax
import jax.numpy as jnp
from jax import lax
from jax.experimental import pallas as pl
from jax.experimental.pallas import tpu as pltpu
from jax.sharding import PartitionSpec as P

HEAD = 128
SLAB = 16
MESH = pl.DeviceIdType.MESH

eps = 1e-05

f32, bf16 = jnp.float32, jnp.bfloat16

GATHER = (
    "gLlo", "gRlo", "gA", "nrm", "nRhi", "gLhi", "nLlo", "gxR", "nLhi", "nA", "nRlo", "gxL", "gRhi",
    "g3A", "oRlo", "oLhi", "P0t", "P0", "oRhi", "oLlo", "g1A", "G0", "G3", "oxL", "nxR", "oxR",
    "P1t", "g2Ahi", "P3t", "nxL", "P3", "P1", "g2Alo", "G1", "zxR", "zxL", "P2t", "P2", "G2",
)
SUMS = (
    "product0", "first0", "product2", "first1", "second0", "second1", "across0", "first2", "norm0",
    "first3", "across1", "relay_y0", "second2", "relay_z0", "sums_y0", "norm1", "second3",
    "across2", "relay_y1", "relay_z1", "across3", "norm2", "sums_y1", "relay_y2", "sums_y2",
    "norm3", "sums_z0", "sums_z1", "relay_y3", "relay_z2", "late_y2", "relay_z3", "late_z0",
    "sums_y3", "sums_z2", "late_y0", "sums_z3", "late_y1", "late_z2", "late_y3", "late_z1",
    "late_z3", "finish0", "finish2", "finish1", "finish3",
)

def dot(a, b, ca, cb):
    return lax.dot_general(a, b, (((ca,), (cb,)), ((), ())), preferred_element_type=f32)


def neighbours():
    place = lax.axis_index("tp")
    x, z, core = place // 4, lax.rem(place // 2, 2), lax.rem(place, 2)
    right = lax.rem(x + 1, 4) * 4 + z * 2 + core
    left = lax.rem(x + 3, 4) * 4 + z * 2 + core
    across = x * 4 + (1 - z) * 2 + core
    twin = x * 4 + z * 2 + (1 - core)
    return x, z, core, {"tp": right}, {"tp": left}, {"tp": across}, {"tp": twin}


def kernel(alpha_ref, saved_ref, gain_ref, grad_ref, pending_ref, wq_ref, wk_ref, wv_ref, wo_ref,
           in_grads_ref, updated_ref,
           normed, grads, weights, out_weights, theirs, heads,
           q_ref, k_ref, v_ref, g_ref, dk_acc, dv_acc,
           back, back_twin, part, xb1, xb2, zb,
           pending, gather, stage, arrived, kept,
           send_sem, recv_sem, load_sem):
    x, z, core, right, left, across, twin = neighbours()
    section = lax.axis_index("section")
    y, zh = section // 4, lax.rem(section, 4)
    rows, depth = saved_ref.shape
    width = wq_ref.shape[1]
    pair, half = 2 * rows, rows // 2
    wide = depth // 2
    narrow = wide // 2
    other = 1 - z

    def at(dy, dz):
        return lax.rem(y + dy + 4, 4) * 4 + lax.rem(zh + dz + 4, 4)

    up = ({"section": at(1, 0)}, {"section": at(0, 1)})
    down = ({"section": at(3, 0)}, {"section": at(0, 3)})

    sends, indices, local = [], iter(range(send_sem.shape[0])), iter(range(load_sem.shape[0]))

    def go(src, dst, to):
        index = next(indices)
        c = pltpu.make_async_remote_copy(
            src_ref=src, dst_ref=dst, send_sem=send_sem.at[index], recv_sem=recv_sem.at[index],
            device_id=to, device_id_type=MESH,
        )
        c.start()
        sends.append(c)
        return c

    def move(src, dst):
        c = pltpu.make_async_copy(src, dst, load_sem.at[next(local)])
        c.start()
        return c

    own_grads = move(grad_ref, grads.at[0, z])
    loads = [
        move(wq_ref, weights.at[0, 0]),
        move(wk_ref, weights.at[0, 1]),
        move(wv_ref, weights.at[0, 2]),
        move(wo_ref, out_weights.at[0]),
    ]
    load_pending = move(pending_ref, pending)

    barrier = pltpu.get_barrier_semaphore()
    friends = (right, left, across, twin) + up + down
    for friend in friends:
        pl.semaphore_signal(barrier, inc=1, device_id=friend, device_id_type=MESH)
    pl.semaphore_wait(barrier, len(friends))

    w_twin = []
    lo, hi = pl.ds(0, half), pl.ds(half, half)
    quarter = [pl.ds(i * SLAB, SLAB) for i in range(rows // SLAB)]
    sent = {}

    def normalize():
        def one(i, carry):
            here = pl.ds(pl.multiple_of(i * 16, 16), 16)
            values = saved_ref[here, :].astype(f32)
            factor = lax.rsqrt(jnp.mean(values * values, axis=-1, keepdims=True) + eps)
            normed[0, z, here, :] = (values * factor * gain_ref[...]).astype(bf16)
            return carry

        lax.fori_loop(0, rows // 16, one, 0)
        for j, w in enumerate((wq_ref, wk_ref, wv_ref)):
            w_twin.append(go(w, weights.at[1, j], twin))
        w_twin.append(go(wo_ref, out_weights.at[1], twin))

    def place_of(r):
        return pl.ds(pl.multiple_of(lax.rem(x + 4 - r, 4) * pair, pair), pair)

    results = []

    def hand_over(r, first, count):
        js, here = pl.ds(first, count), place_of(r)
        results.append(go(theirs.at[js, here], heads.at[core, js, here], twin))

    def project(r, which):
        if r == 0:
            for c in (w_twin if which else loads)[:3]:
                c.wait_recv() if which else c.wait()
        here = place_of(r)

        def one(j, carry):
            product = dot(normed[r].reshape(pair, depth), weights[which, j], 1, 0).astype(bf16)
            if which == 0:
                heads[core, j, here, :] = product
            else:
                theirs[j, here, :] = product
            return carry

        lax.fori_loop(0, 3, one, 0)
        if which == 1:
            hand_over(r, 0, 3)

    def project_grads(r):
        if r == 0:
            own_grads.wait()
            loads[3].wait()
            w_twin[3].wait_recv()
        here = place_of(r)
        for which in (1, 0):
            product = dot(grads[r].reshape(pair, depth), out_weights[which], 1, 1).astype(bf16)
            if which == 0:
                heads[core, 3, here, :] = product
            else:
                theirs[3, here, :] = product
                hand_over(r, 3, 1)

    mine, crossed = normed.at[0, z], normed.at[0, other]
    moves = {
        "gA": ((), grad_ref, grads.at[0, z], across),
        "nA": ((), mine, mine, across),
        "gxR": (("gRlo",), grads.at[1, z, lo], grads.at[2, z, lo], right),
        "gxL": (("gLhi",), grads.at[3, z, hi], grads.at[2, z, hi], left),
        "nxR": (("nRlo",), normed.at[1, z, lo], normed.at[2, z, lo], right),
        "nxL": (("nLhi",), normed.at[3, z, hi], normed.at[2, z, hi], left),
        "oxR": (("oRlo",), normed.at[1, other, lo], normed.at[2, other, lo], right),
        "oxL": (("oLhi",), normed.at[3, other, hi], normed.at[2, other, hi], left),
        "g1A": (("gRlo", "gRhi"), grads.at[1, z], grads.at[1, z], across),
        "g3A": (("gLlo", "gLhi"), grads.at[3, z], grads.at[3, z], across),
        "g2Alo": (("gxR",), grads.at[2, z, quarter[1]], grads.at[2, z, quarter[1]], across),
        "g2Ahi": (("gxL",), grads.at[2, z, quarter[2]], grads.at[2, z, quarter[2]], across),
        "zxR": (("g1A",), grads.at[1, other, quarter[0]], grads.at[2, other, quarter[0]], right),
        "zxL": (("g3A",), grads.at[3, other, quarter[3]], grads.at[2, other, quarter[3]], left),
    }
    for end, part_rows in (("lo", lo), ("hi", hi)):
        for way, r, to in (("R", 1, right), ("L", 3, left)):
            moves["g" + way + end] = ((), grad_ref.at[part_rows], grads.at[r, z, part_rows], to)
            moves["n" + way + end] = ((), mine.at[part_rows], normed.at[r, z, part_rows], to)
            moves["o" + way + end] = (("nA",), crossed.at[part_rows], normed.at[r, other, part_rows], to)
    needs = {
        "P0": ("nA",), "P1": ("nRlo", "nRhi", "oRlo", "oRhi"), "P3": ("nLlo", "nLhi", "oLlo", "oLhi"),
        "P2": ("nxR", "nxL", "oxR", "oxL"), "G0": ("gA",), "G1": ("gRlo", "gRhi", "g1A"),
        "G3": ("gLlo", "gLhi", "g3A"), "G2": ("gxR", "gxL", "g2Alo", "g2Ahi", "zxR", "zxL"),
    }
    landed = set()

    def need(names):
        for name in names:
            if name not in landed:
                landed.add(name)
                sent[name].wait_recv()

    for name in GATHER:
        if name == "nrm":
            normalize()
        elif name in moves:
            waits, src, dst, to = moves[name]
            need(waits)
            sent[name] = go(src, dst, to)
        else:
            need(needs[name[:2]])
            if name[0] == "P":
                project(int(name[1]), 1 if name.endswith("t") else 0)
            else:
                project_grads(int(name[1]))
    for c in results:
        c.wait_recv()

    tokens = q_ref.shape[0]
    block = 256
    chips = tokens // pair
    scale = 1.0 / math.sqrt(HEAD)
    places = [(chip, c) for chip in range(chips) for c in (0, 1)]
    for j, ref in enumerate((q_ref, k_ref, v_ref, g_ref)):
        for chip, c in places:
            ref[pl.ds((2 * chip + c) * rows, rows), :] = heads[c, j, pl.ds(chip * rows, rows), :]
    below = lax.broadcasted_iota(jnp.int32, (block, block), 0) <= lax.broadcasted_iota(
        jnp.int32, (block, block), 1
    )

    def put(j, chip, c, cols, value):
        for s in range(rows // SLAB):
            there = pl.ds((s * chips + chip) * SLAB, SLAB)
            back[c, j, there, cols] = value[s * SLAB : (s + 1) * SLAB].astype(bf16)

    swaps = []
    for head in range(width // HEAD):
        cols = pl.ds(head * HEAD, HEAD)
        keys_t = k_ref[:, cols].T
        values_t = v_ref[:, cols].T
        for step in reversed(range(tokens // block)):
            n = (step + 1) * block
            mine = pl.ds(step * block, block)
            query, grad = q_ref[mine, cols], g_ref[mine, cols]
            scores = dot(k_ref[pl.ds(0, n), cols], query, 1, 1) * (scale * math.log2(math.e))
            last = jnp.where(below, scores[n - block :], -1e30)
            scores = last if step == 0 else jnp.concatenate((scores[: n - block], last), axis=0)
            peak = jnp.max(scores, axis=0, keepdims=True)
            exps = jnp.exp2(scores - peak)
            exps = exps * (1.0 / jnp.sum(exps, axis=0, keepdims=True))
            probs = exps.astype(bf16)
            output_t = dot(values_t[:, :n], probs, 1, 0)
            delta = jnp.sum(grad.astype(f32).T * output_t, axis=0, keepdims=True)
            grad_probs = dot(v_ref[pl.ds(0, n), cols], grad, 1, 1)
            grad_scores = (exps * ((grad_probs - delta) * scale)).astype(bf16)
            grad_query = dot(keys_t[:, :n], grad_scores, 1, 0).T
            for chip, c in places:
                offset = (2 * chip + c) * rows - step * block
                if 0 <= offset < block:
                    put(0, chip, c, cols, grad_query[offset : offset + rows])
            more_k = dot(grad_scores, query, 1, 0)
            more_v = dot(probs, grad, 1, 0)
            if step == tokens // block - 1:
                dk_acc[...] = more_k
                dv_acc[...] = more_v
            else:
                dk_acc[pl.ds(0, n)] += more_k
                dv_acc[pl.ds(0, n)] += more_v
        for j, acc in ((1, dk_acc), (2, dv_acc)):
            for chip, c in places:
                put(j, chip, c, cols, acc[pl.ds((2 * chip + c) * rows, rows), :])
        everything = pl.ds(0, tokens // 2)
        swaps.append(go(back.at[1 - core, :, everything, cols], back_twin.at[:, everything, cols], twin))

    slabs = rows // SLAB
    chunk = 512
    together = chips * SLAB

    def coefficient(j, s):
        return jnp.where(s > j, alpha_ref[s, j], 0.0)

    coeffs = {}
    for r in range(4):
        for t in range(4):
            coeffs[0, r, t] = coefficient(at(0, r), at(4 - t, 0))
            coeffs[1, r, t] = coefficient(at(r, 0), at(0, 4 - t))

    def spot(r):
        return lax.rem(x + r, 4)

    def plus(target, source):
        target[...] = (target[...].astype(f32) + source[...].astype(f32)).astype(bf16)

    live = {}

    def product(s):
        here = pl.ds(s * together, 2 * together)

        def step(n, carry):
            cols = pl.ds(pl.multiple_of(n * chunk, chunk), chunk)
            total = dot(back[core, 0, here, :], weights[0, 0, cols, :], 1, 1)
            for j in (1, 2):
                total += dot(back[core, j, here, :], weights[0, j, cols, :], 1, 1)
            for j in (0, 1, 2):
                total += dot(back_twin[j, here, :], weights[1, j, cols, :], 1, 1)
            part[s : s + 2, :, :, :, cols] = total.astype(bf16).reshape(2, chips // 2, 2, SLAB, chunk)
            return carry

        lax.fori_loop(0, depth // chunk, step, 0)

    def first(s):
        live["x1r", s] = go(part.at[s, spot(2), 0], xb1.at[s, 0], right)
        live["x1l", s] = go(part.at[s, spot(2), 1], xb1.at[s, 1], left)
        live["x2", s] = [
            go(part.at[s, spot(1), 1], xb2.at[s, 0, 1], right),
            go(part.at[s, spot(3), 0], xb2.at[s, 1, 0], left),
        ]

    def second(s):
        live["x1r", s].wait_recv()
        plus(part.at[s, spot(1), 0], xb1.at[s, 0])
        live["x2", s].append(go(part.at[s, spot(1), 0], xb2.at[s, 0, 0], right))
        live["x1l", s].wait_recv()
        plus(part.at[s, spot(3), 1], xb1.at[s, 1])
        live["x2", s].append(go(part.at[s, spot(3), 1], xb2.at[s, 1, 1], left))

    def cross(s):
        for c in live["x2", s]:
            c.wait_recv()
        total = part[s, x, other].astype(f32) + xb2[s, 0, other].astype(f32) + xb2[s, 1, other].astype(f32)
        part[s, x, other] = total.astype(bf16)
        live["z", s] = go(part.at[s, x, other], zb.at[s], across)

    def norm_back(s):
        live["z", s].wait_recv()
        here = pl.ds(s * SLAB, SLAB)
        saved = saved_ref[here, :].astype(f32)
        total = part[s, x, z].astype(f32) + xb2[s, 0, z].astype(f32)
        total = total + xb2[s, 1, z].astype(f32) + zb[s].astype(f32)
        factor = lax.rsqrt(jnp.mean(saved * saved, axis=-1, keepdims=True) + eps)
        scaled = total * gain_ref[...]
        inner = jnp.mean(scaled * saved, axis=-1, keepdims=True)
        change = factor * (scaled - saved * (factor * factor * inner))
        value = (grads[0, z, here, :].astype(f32) + change).astype(bf16)
        in_grads_ref[here, :] = value
        for w in (0, 1):
            source = in_grads_ref.at[here, pl.ds(w * wide, wide)]
            live["g", s, w] = (
                go(source, gather.at[s, w, 0], up[w]),
                go(source, gather.at[s, w, 2], down[w]),
            )

    lower, upper = pl.ds(0, narrow), pl.ds(narrow, narrow)
    all_rows = pl.ds(0, SLAB)

    def relay(s, w):
        one, three = live["g", s, w]
        one.wait_recv()
        a = go(gather.at[s, w, 0, all_rows, lower], gather.at[s, w, 1, all_rows, lower], up[w])
        three.wait_recv()
        b = go(gather.at[s, w, 2, all_rows, upper], gather.at[s, w, 1, all_rows, upper], down[w])
        live["r", s, w] = (a, b)

    def sums(s, w):
        for c in live["r", s, w]:
            c.wait_recv()

        def body(i, carry):
            cols = pl.ds(pl.multiple_of(i * 256, 256), 256)
            own = pl.ds(pl.multiple_of(w * wide + i * 256, 256), 256)
            blocks = [in_grads_ref[pl.ds(s * SLAB, SLAB), own].astype(f32)]
            blocks += [gather[s, w, t, :, cols].astype(f32) for t in range(3)]
            for r in range(4):
                total = blocks[0] * coeffs[w, r, 0]
                for t in (1, 2, 3):
                    total = total + blocks[t] * coeffs[w, r, t]
                if r == 0:
                    kept[s, w, :, cols] = total
                else:
                    stage[s, w, r - 1, :, cols] = total.astype(bf16)
            return carry

        lax.fori_loop(0, wide // 256, body, 0)
        u, d = up[1 - w], down[1 - w]
        live["p", s, w] = (
            go(stage.at[s, w, 1, all_rows, lower], arrived.at[s, w, 2, all_rows, lower], u),
            go(stage.at[s, w, 1, all_rows, upper], arrived.at[s, w, 2, all_rows, upper], d),
        )
        live["q", s, w] = [
            go(stage.at[s, w, 0, all_rows, upper], arrived.at[s, w, 0, all_rows, upper], u),
            go(stage.at[s, w, 2, all_rows, lower], arrived.at[s, w, 1, all_rows, lower], d),
        ]

    def late(s, w):
        a, b = live["p", s, w]
        u, d = up[1 - w], down[1 - w]
        a.wait_recv()
        plus(stage.at[s, w, 0, all_rows, lower], arrived.at[s, w, 2, all_rows, lower])
        live["q", s, w].append(
            go(stage.at[s, w, 0, all_rows, lower], arrived.at[s, w, 0, all_rows, lower], u)
        )
        b.wait_recv()
        plus(stage.at[s, w, 2, all_rows, upper], arrived.at[s, w, 2, all_rows, upper])
        live["q", s, w].append(
            go(stage.at[s, w, 2, all_rows, upper], arrived.at[s, w, 1, all_rows, upper], d)
        )

    def finish(s):
        here = pl.ds(s * SLAB, SLAB)
        for w in (1, 0):
            for c in live["q", s, w]:
                c.wait_recv()
            cols = pl.ds(w * wide, wide)
            total = pending[here, cols].astype(f32) + kept[s, w]
            total = total + arrived[s, w, 0].astype(f32) + arrived[s, w, 1].astype(f32)
            updated_ref[here, cols] = total.astype(bf16)

    stages = {
        "product": product, "first": first, "second": second, "across": cross, "norm": norm_back,
        "relay_y": lambda s: relay(s, 0), "relay_z": lambda s: relay(s, 1),
        "sums_y": lambda s: sums(s, 0), "sums_z": lambda s: sums(s, 1),
        "late_y": lambda s: late(s, 0), "late_z": lambda s: late(s, 1), "finish": finish,
    }
    for c in swaps:
        c.wait_recv()
    load_pending.wait()
    for name in SUMS:
        stages[name[:-1]](int(name[-1]))
    for c in sends:
        c.wait_send()


def on_device(saved_in, out_grad, pending, gain, alpha, w_query, w_key, w_value, w_out):
    _, rows, depth = saved_in.shape
    width = w_query.shape[2]
    tokens = 16 * rows
    slabs = rows // SLAB
    wide = depth // 2
    vmem = pl.BlockSpec(memory_space=pltpu.VMEM)
    smem = pl.BlockSpec(memory_space=pltpu.SMEM)
    hbm = pl.BlockSpec(memory_space=pl.ANY)
    rows_out = jax.ShapeDtypeStruct((rows, depth), bf16)

    def buffer(*shape):
        return pltpu.VMEM(shape, bf16)

    grad_input, updated = pl.pallas_call(
        kernel,
        out_shape=(rows_out, rows_out),
        in_specs=[smem, vmem, vmem, hbm, hbm, hbm, hbm, hbm, hbm],
        out_specs=(vmem, vmem),
        scratch_shapes=[
            buffer(4, 2, rows, depth),
            buffer(4, 2, rows, depth),
            buffer(2, 3, depth, width),
            buffer(2, width, depth),
            buffer(4, tokens // 2, width),
            buffer(2, 4, tokens // 2, width),
            buffer(tokens, width),
            buffer(tokens, width),
            buffer(tokens, width),
            buffer(tokens, width),
            pltpu.VMEM((tokens, HEAD), f32),
            pltpu.VMEM((tokens, HEAD), f32),
            buffer(2, 3, tokens // 2, width),
            buffer(3, tokens // 2, width),
            buffer(slabs, 4, 2, SLAB, depth),
            buffer(slabs, 2, SLAB, depth),
            buffer(slabs, 2, 2, SLAB, depth),
            buffer(slabs, SLAB, depth),
            buffer(rows, depth),
            buffer(slabs, 2, 3, SLAB, wide),
            buffer(slabs, 2, 3, SLAB, wide),
            buffer(slabs, 2, 3, SLAB, wide),
            pltpu.VMEM((slabs, 2, SLAB, wide), f32),
            pltpu.SemaphoreType.DMA((40 + 27 * slabs,)),
            pltpu.SemaphoreType.DMA((40 + 27 * slabs,)),
            pltpu.SemaphoreType.DMA((6,)),
        ],
        compiler_params=pltpu.CompilerParams(
            collective_id=1, has_side_effects=True, vmem_limit_bytes=52 * 2**20
        ),
        cost_estimate=pl.CostEstimate(flops=14 * 10**9, bytes_accessed=10**7, transcendentals=10**6),
    )(alpha, saved_in[0], gain, out_grad[0], pending[0], w_query[0], w_key[0], w_value[0], w_out[0])
    return (grad_input[None], updated[None])


def solution(mesh):
    return jax.shard_map(
        on_device,
        mesh=mesh,
        in_specs=(
            P("section", "tp", None),
            P("section", "tp", None),
            P("section", "tp", None),
            P("section", None),
            P(),
            P("section", None, "tp"),
            P("section", None, "tp"),
            P("section", None, "tp"),
            P("section", "tp", None),
        ),
        out_specs=(P("section", "tp", None), P("section", "tp", None)),
        check_vma=False,
    )
```

time: 401 us -> 137 us (0.34)
  waiting for transfers between devices: 269 us -> 0 us
  Pallas kernels: 0 us -> 130 us
  matrix products: 62.5 us -> 0 us
  other arithmetic: 43.7 us -> 0 us
  between operations: 14 us -> 0.65 us
  local copies, waits for them, and re-layouts: 10.2 us -> 5.88 us
    all_gather x3 -> x0, waiting for transfers between devices: 186 us -> none  [the longest x1 95.2 us: on_device(): arrived = lax.all_gather(grad_input[None], 'section', axis=0, tiled=True)]
    pallas_call x0 -> x1, Pallas kernels: none -> 130 us  [on_device(): pl.pallas_call(kernel, out_shape=(rows_out, rows_out), in_specs=[smem, vm...]
    reduce_scatter x1 -> x0, waiting for transfers between devices: 81.3 us -> none  [on_device(): lax.psum_scatter(total.astype(jnp.bfloat16), 'tp', scatter_dimension=0, t...]
    dot_general x12 -> x0, matrix products: 54.4 us -> none  [the longest x3 24.8 us: on_device(): jnp.einsum('te,de->td', grad_part, weight, preferred_element_type=jnp.flo...]
    add x16 -> x0, other arithmetic: 29.1 us -> none  [add_one(): return total + coeffs[source] * arrived[source].astype(jnp.float32)]
    dynamic_slice x17 -> x0, local copies, waits for them, and re-layouts: 9.91 us -> none  [the longest x16 9.73 us: add_one(): return total + coeffs[source] * arrived[source].astype(jnp.float32)]
    sub x1 -> x0, matrix products: 8.15 us -> none  [attend_back(): weights = jnp.exp(scores - peak)]
    convert_element_type x3 -> x0, other arithmetic: 7.09 us -> none  [the longest x1 4.98 us: attend_back(): probs = weights.astype(jnp.bfloat16)]
  transfers between devices with their start and end apart: 4 -> 0, of which waited for: 4 -> 0; matrix products, arithmetic and copies ran while one was open for 1% -> 0% of each run, Pallas kernels for 0% -> 0%
where the time goes in v3:
time: 137 us
  Pallas kernels  130 us (95%)
  local copies, waits for them, and re-layouts  5.88 us (4%)
    pallas_call x1, Pallas kernels, on_device(): pl.pallas_call(kernel, out_shape=(rows_out, rows_out), in_specs=[smem, vm...  130 us
    unnamed x12, local copies, waits for them, and re-layouts  5.88 us

profile of v3, /device:TPU:8, one launch (start us, length us, event | category | flops | bytes accessed | tf_op | source)
XLA Modules:
  0.0 136.6 jit_solution(10652328611169854895)
XLA Ops:
  0.6 0.0 copy-start
  0.6 1.0 copy-done
  1.6 0.0 copy-start.1
  1.6 1.0 copy-done.1
  2.6 0.0 copy-start.2
  2.6 1.0 copy-done.2
  3.6 0.0 copy-start.3
  3.6 0.7 copy-done.3
  4.3 0.0 copy-start.4
  4.3 0.7 copy-done.4
  5.0 130.1 %shard_map.104 = (bf16[64,3072]{1,0:T(8,128)(2,1)S(1)}, bf16[64,3072]{1,0:T(8,128)(2,1)S(1)}) custom-call(f32[16,16]{1,0:T(8,128)S(1)} %copy-done.4, bf16[64,3072]{1,0:T(8,128)(2,1)S(1)} %bitcast.11, f32[1,3072]{1,0:T(1,128)S(1)} %copy-done.3, bf16[64,3072]{1,0:T(8,128)(2,1)S(1)} %bitcast.12, bf16[64,3072]{1,0:T(8,128)(2,1)S(1)} %bitcast.13, ...), custom_call_target="tpu_custom_call" | custom-call | flops 14000000000 | bytes 10000000 | tf_op jit(solution)/shard_map/pallas_call | solution.py:439
  135.1 0.7 copy.13
  135.9 0.7 copy.14
Async XLA Ops:
  0.6 1.0 copy-start
  1.6 1.0 copy-start.1
  2.6 1.0 copy-start.2
  3.6 0.7 copy-start.3
  4.3 0.7 copy-start.4

commit v4 on v3

--- a/solution.py
+++ b/solution.py
@@ -21,13 +21,15 @@
     "P1t", "g2Ahi", "P3t", "nxL", "P3", "P1", "g2Alo", "G1", "zxR", "zxL", "P2t", "P2", "G2",
 )
 SUMS = (
-    "product0", "first0", "product2", "first1", "second0", "second1", "across0", "first2", "norm0",
-    "first3", "across1", "relay_y0", "second2", "relay_z0", "sums_y0", "norm1", "second3",
-    "across2", "relay_y1", "relay_z1", "across3", "norm2", "sums_y1", "relay_y2", "sums_y2",
-    "norm3", "sums_z0", "sums_z1", "relay_y3", "relay_z2", "late_y2", "relay_z3", "late_z0",
-    "sums_y3", "sums_z2", "late_y0", "sums_z3", "late_y1", "late_z2", "late_y3", "late_z1",
-    "late_z3", "finish0", "finish2", "finish1", "finish3",
+    "product0", "first1", "first0", "product2", "second1", "across1", "second0", "across0", "norm1",
+    "first2", "norm0", "relay_z1", "relay_y1", "first3", "relay_y0", "sums_y1", "second2",
+    "relay_z0", "sums_z1", "sums_y0", "second3", "across2", "sums_z0", "late_z1", "across3",
+    "norm2", "late_z0", "norm3", "relay_z2", "relay_y3", "relay_y2", "late_y1", "relay_z3",
+    "sums_y3", "sums_z2", "sums_y2", "sums_z3", "finish1", "late_y3", "late_y0", "late_z2",
+    "late_y2", "late_z3", "finish0", "finish3", "finish2",
 )
+ACROSS_FIRST = (0,)
+
 
 def dot(a, b, ca, cb):
     return lax.dot_general(a, b, (((ca,), (cb,)), ((), ())), preferred_element_type=f32)
@@ -43,11 +45,11 @@
     return x, z, core, {"tp": right}, {"tp": left}, {"tp": across}, {"tp": twin}
 
 
-def kernel(alpha_ref, saved_ref, gain_ref, grad_ref, pending_ref, wq_ref, wk_ref, wv_ref, wo_ref,
+def kernel(alpha_in, saved_in, gain_in, grad_ref, pending_ref, wq_ref, wk_ref, wv_ref, wo_ref,
            in_grads_ref, updated_ref,
-           normed, grads, weights, out_weights, theirs, heads,
+           alpha_ref, saved_ref, gain_ref, normed, grads, weights, out_weights, theirs, heads,
            q_ref, k_ref, v_ref, g_ref, dk_acc, dv_acc,
-           back, back_twin, part, xb1, xb2, zb,
+           back, back_twin, part, xb1, xb2, za, zb,
            pending, gather, stage, arrived, kept,
            send_sem, recv_sem, load_sem):
     x, z, core, right, left, across, twin = neighbours()
@@ -83,6 +85,7 @@
         c.start()
         return c
 
+    load_rows = [move(saved_in, saved_ref), move(gain_in, gain_ref)]
     own_grads = move(grad_ref, grads.at[0, z])
     loads = [
         move(wq_ref, weights.at[0, 0]),
@@ -90,7 +93,7 @@
         move(wv_ref, weights.at[0, 2]),
         move(wo_ref, out_weights.at[0]),
     ]
-    load_pending = move(pending_ref, pending)
+    load_late = [move(pending_ref, pending), move(alpha_in, alpha_ref)]
 
     barrier = pltpu.get_barrier_semaphore()
     friends = (right, left, across, twin) + up + down
@@ -104,6 +107,9 @@
     sent = {}
 
     def normalize():
+        for c in load_rows:
+            c.wait()
+
         def one(i, carry):
             here = pl.ds(pl.multiple_of(i * 16, 16), 16)
             values = saved_ref[here, :].astype(f32)
@@ -209,7 +215,7 @@
         c.wait_recv()
 
     tokens = q_ref.shape[0]
-    block = 256
+    block = 512
     chips = tokens // pair
     scale = 1.0 / math.sqrt(HEAD)
     places = [(chip, c) for chip in range(chips) for c in (0, 1)]
@@ -265,12 +271,15 @@
         swaps.append(go(back.at[1 - core, :, everything, cols], back_twin.at[:, everything, cols], twin))
 
     slabs = rows // SLAB
+    all_rows = pl.ds(0, SLAB)
     chunk = 512
     together = chips * SLAB
 
     def coefficient(j, s):
         return jnp.where(s > j, alpha_ref[s, j], 0.0)
 
+    for c in load_late:
+        c.wait()
     coeffs = {}
     for r in range(4):
         for t in range(4):
@@ -300,7 +309,13 @@
 
         lax.fori_loop(0, depth // chunk, step, 0)
 
+    early, latter = pl.ds(0, wide), pl.ds(wide, wide)
+
     def first(s):
+        if s in ACROSS_FIRST:
+            for r in (2, 1, 3, 0):
+                live["za", s, r] = go(part.at[s, spot(r), other], za.at[r], across)
+            return
         live["x1r", s] = go(part.at[s, spot(2), 0], xb1.at[s, 0], right)
         live["x1l", s] = go(part.at[s, spot(2), 1], xb1.at[s, 1], left)
         live["x2", s] = [
@@ -309,6 +324,19 @@
         ]
 
     def second(s):
+        if s in ACROSS_FIRST:
+            two, one, three = (part.at[s, spot(r), z] for r in (2, 1, 3))
+            live["za", s, 2].wait_recv()
+            plus(two, za.at[2])
+            live["x1r", s] = go(two.at[all_rows, early], xb1.at[s, 0, all_rows, early], right)
+            live["x1l", s] = go(two.at[all_rows, latter], xb1.at[s, 0, all_rows, latter], left)
+            live["za", s, 1].wait_recv()
+            plus(one, za.at[1])
+            live["x2", s] = [go(one.at[all_rows, latter], xb2.at[s, 0, 0, all_rows, latter], right)]
+            live["za", s, 3].wait_recv()
+            plus(three, za.at[3])
+            live["x2", s].append(go(three.at[all_rows, early], xb2.at[s, 1, 0, all_rows, early], left))
+            return
         live["x1r", s].wait_recv()
         plus(part.at[s, spot(1), 0], xb1.at[s, 0])
         live["x2", s].append(go(part.at[s, spot(1), 0], xb2.at[s, 0, 0], right))
@@ -317,6 +345,15 @@
         live["x2", s].append(go(part.at[s, spot(3), 1], xb2.at[s, 1, 1], left))
 
     def cross(s):
+        if s in ACROSS_FIRST:
+            one, three = (part.at[s, spot(r), z] for r in (1, 3))
+            live["x1r", s].wait_recv()
+            plus(one.at[all_rows, early], xb1.at[s, 0, all_rows, early])
+            live["x2", s].append(go(one.at[all_rows, early], xb2.at[s, 0, 0, all_rows, early], right))
+            live["x1l", s].wait_recv()
+            plus(three.at[all_rows, latter], xb1.at[s, 0, all_rows, latter])
+            live["x2", s].append(go(three.at[all_rows, latter], xb2.at[s, 1, 0, all_rows, latter], left))
+            return
         for c in live["x2", s]:
             c.wait_recv()
         total = part[s, x, other].astype(f32) + xb2[s, 0, other].astype(f32) + xb2[s, 1, other].astype(f32)
@@ -324,11 +361,16 @@
         live["z", s] = go(part.at[s, x, other], zb.at[s], across)
 
     def norm_back(s):
-        live["z", s].wait_recv()
         here = pl.ds(s * SLAB, SLAB)
+        if s in ACROSS_FIRST:
+            for c in live["x2", s] + [live["za", s, 0]]:
+                c.wait_recv()
+        else:
+            live["z", s].wait_recv()
         saved = saved_ref[here, :].astype(f32)
-        total = part[s, x, z].astype(f32) + xb2[s, 0, z].astype(f32)
-        total = total + xb2[s, 1, z].astype(f32) + zb[s].astype(f32)
+        last, k = (za[0], 0) if s in ACROSS_FIRST else (zb[s], z)
+        total = part[s, x, z].astype(f32) + xb2[s, 0, k].astype(f32)
+        total = total + xb2[s, 1, k].astype(f32) + last.astype(f32)
         factor = lax.rsqrt(jnp.mean(saved * saved, axis=-1, keepdims=True) + eps)
         scaled = total * gain_ref[...]
         inner = jnp.mean(scaled * saved, axis=-1, keepdims=True)
@@ -343,7 +385,6 @@
             )
 
     lower, upper = pl.ds(0, narrow), pl.ds(narrow, narrow)
-    all_rows = pl.ds(0, SLAB)
 
     def relay(s, w):
         one, three = live["g", s, w]
@@ -415,7 +456,6 @@
     }
     for c in swaps:
         c.wait_recv()
-    load_pending.wait()
     for name in SUMS:
         stages[name[:-1]](int(name[-1]))
     for c in sends:
@@ -429,9 +469,8 @@
     slabs = rows // SLAB
     wide = depth // 2
     vmem = pl.BlockSpec(memory_space=pltpu.VMEM)
-    smem = pl.BlockSpec(memory_space=pltpu.SMEM)
-    hbm = pl.BlockSpec(memory_space=pl.ANY)
-    rows_out = jax.ShapeDtypeStruct((rows, depth), bf16)
+    hbm = pl.BlockSpec(memory_space=pltpu.HBM)
+    rows_out = pltpu.VMEM((rows, depth), bf16)
 
     def buffer(*shape):
         return pltpu.VMEM(shape, bf16)
@@ -439,9 +478,12 @@
     grad_input, updated = pl.pallas_call(
         kernel,
         out_shape=(rows_out, rows_out),
-        in_specs=[smem, vmem, vmem, hbm, hbm, hbm, hbm, hbm, hbm],
+        in_specs=[hbm] * 9,
         out_specs=(vmem, vmem),
         scratch_shapes=[
+            pltpu.SMEM(alpha.shape, f32),
+            buffer(rows, depth),
+            pltpu.VMEM((1, depth), f32),
             buffer(4, 2, rows, depth),
             buffer(4, 2, rows, depth),
             buffer(2, 3, depth, width),
@@ -459,21 +501,23 @@
             buffer(slabs, 4, 2, SLAB, depth),
             buffer(slabs, 2, SLAB, depth),
             buffer(slabs, 2, 2, SLAB, depth),
+            buffer(4, SLAB, depth),
             buffer(slabs, SLAB, depth),
             buffer(rows, depth),
             buffer(slabs, 2, 3, SLAB, wide),
             buffer(slabs, 2, 3, SLAB, wide),
             buffer(slabs, 2, 3, SLAB, wide),
             pltpu.VMEM((slabs, 2, SLAB, wide), f32),
-            pltpu.SemaphoreType.DMA((40 + 27 * slabs,)),
-            pltpu.SemaphoreType.DMA((40 + 27 * slabs,)),
-            pltpu.SemaphoreType.DMA((6,)),
+            pltpu.SemaphoreType.DMA((43 + 27 * slabs,)),
+            pltpu.SemaphoreType.DMA((43 + 27 * slabs,)),
+            pltpu.SemaphoreType.DMA((9,)),
         ],
         compiler_params=pltpu.CompilerParams(
-            collective_id=1, has_side_effects=True, vmem_limit_bytes=52 * 2**20
+            collective_id=1, has_side_effects=True, vmem_limit_bytes=56 * 2**20
         ),
         cost_estimate=pl.CostEstimate(flops=14 * 10**9, bytes_accessed=10**7, transcendentals=10**6),
-    )(alpha, saved_in[0], gain, out_grad[0], pending[0], w_query[0], w_key[0], w_value[0], w_out[0])
+    )(*(pltpu.with_memory_space_constraint(a, pltpu.HBM) for a in (
+        alpha, saved_in[0], gain, out_grad[0], pending[0], w_query[0], w_key[0], w_value[0], w_out[0])))
     return (grad_input[None], updated[None])
 
 

time: 137 us -> 122 us (0.89)
  Pallas kernels: 130 us -> 119 us
  local copies, waits for them, and re-layouts: 5.88 us -> 1.49 us
    pallas_call x1, Pallas kernels: 130 us -> 119 us  [on_device(): pl.pallas_call(kernel, out_shape=(rows_out, rows_out), in_specs=[hbm] * 9...]
    unnamed x12 -> x2, local copies, waits for them, and re-layouts: 5.88 us -> 1.49 us
where the time goes in v4:
time: 122 us; the launch traced here: 121 us
  Pallas kernels  119 us (98%)
  local copies, waits for them, and re-layouts  1.49 us (1%)
    pallas_call x1, Pallas kernels, on_device(): pl.pallas_call(kernel, out_shape=(rows_out, rows_out), in_specs=[hbm] * 9...  119 us

profile of v4, /device:TPU:8, one launch (start us, length us, event | category | flops | bytes accessed | tf_op | source)
XLA Modules:
  0.0 121.5 jit_solution(9511662341179186647)
XLA Ops:
  0.6 119.3 %shard_map.104 = (bf16[64,3072]{1,0:T(8,128)(2,1)S(1)}, bf16[64,3072]{1,0:T(8,128)(2,1)S(1)}) custom-call(f32[16,16]{1,0:T(8,128)} %alpha_in.1, bf16[64,3072]{1,0:T(8,128)(2,1)} %bitcast.15, f32[1,3072]{1,0:T(1,128)} %gain_in.1, bf16[64,3072]{1,0:T(8,128)(2,1)} %bitcast.16, bf16[64,3072]{1,0:T(8,128)(2,1)} %bitcast.17, bf16[3072,256]{1,0:T(8,128)(2,1)} %bitcast.11, ...), custom_call_target="tpu_custom_call" | custom-call | flops 14000000000 | bytes 10000000 | tf_op jit(solution)/shard_map/pallas_call | solution.py:478
  120.0 0.7 copy.13
  120.7 0.7 copy.14

commit v5 on v4

--- a/solution.py
+++ b/solution.py
@@ -18,15 +18,15 @@
 GATHER = (
     "gLlo", "gRlo", "gA", "nrm", "nRhi", "gLhi", "nLlo", "gxR", "nLhi", "nA", "nRlo", "gxL", "gRhi",
     "g3A", "oRlo", "oLhi", "P0t", "P0", "oRhi", "oLlo", "g1A", "G0", "G3", "oxL", "nxR", "oxR",
-    "P1t", "g2Ahi", "P3t", "nxL", "P3", "P1", "g2Alo", "G1", "zxR", "zxL", "P2t", "P2", "G2",
+    "P1t", "g2Ahi", "P3t", "nxL", "P3", "P1", "g2Alo", "G1", "zxR", "zxL", "P2t", "P2", "G2", "S",
 )
 SUMS = (
-    "product0", "first1", "first0", "product2", "second1", "across1", "second0", "across0", "norm1",
-    "first2", "norm0", "relay_z1", "relay_y1", "first3", "relay_y0", "sums_y1", "second2",
-    "relay_z0", "sums_z1", "sums_y0", "second3", "across2", "sums_z0", "late_z1", "across3",
-    "norm2", "late_z0", "norm3", "relay_z2", "relay_y3", "relay_y2", "late_y1", "relay_z3",
-    "sums_y3", "sums_z2", "sums_y2", "sums_z3", "finish1", "late_y3", "late_y0", "late_z2",
-    "late_y2", "late_z3", "finish0", "finish3", "finish2",
+    "producta0", "firsta0", "firsta1", "productb0", "firstb0", "firstb1", "product2", "second1",
+    "second0", "across1", "across0", "first2", "norm1", "relay_y1", "norm0", "first3", "sums_y1",
+    "relay_z1", "relay_y0", "second2", "sums_y0", "relay_z0", "second3", "across2", "across3",
+    "sums_z1", "norm2", "norm3", "sums_z0", "relay_z2", "relay_y2", "late_z1", "late_y0",
+    "relay_z3", "relay_y3", "sums_y2", "sums_z2", "sums_y3", "late_z0", "sums_z3", "late_y2",
+    "late_y1", "late_z2", "late_y3", "finish0", "late_z3", "finish1", "finish2", "finish3",
 )
 ACROSS_FIRST = (0,)
 
@@ -48,7 +48,7 @@
 def kernel(alpha_in, saved_in, gain_in, grad_ref, pending_ref, wq_ref, wk_ref, wv_ref, wo_ref,
            in_grads_ref, updated_ref,
            alpha_ref, saved_ref, gain_ref, normed, grads, weights, out_weights, theirs, heads,
-           q_ref, k_ref, v_ref, g_ref, dk_acc, dv_acc,
+           q_ref, k_ref, v_ref, g_ref, probs_f, outputs, dk_acc, dv_acc, own_sums,
            back, back_twin, part, xb1, xb2, za, zb,
            pending, gather, stage, arrived, kept,
            send_sem, recv_sem, load_sem):
@@ -190,6 +190,40 @@
         "P2": ("nxR", "nxL", "oxR", "oxL"), "G0": ("gA",), "G1": ("gRlo", "gRhi", "g1A"),
         "G3": ("gLlo", "gLhi", "g3A"), "G2": ("gxR", "gxL", "g2Alo", "g2Ahi", "zxR", "zxL"),
     }
+    tokens = q_ref.shape[0]
+    block = 512
+    chips = tokens // pair
+    scale = 1.0 / math.sqrt(HEAD)
+    places = [(chip, c) for chip in range(chips) for c in (0, 1)]
+    below = lax.broadcasted_iota(jnp.int32, (block, block), 0) <= lax.broadcasted_iota(
+        jnp.int32, (block, block), 1
+    )
+
+    def assemble(j, ref):
+        for chip, c in places:
+            ref[pl.ds((2 * chip + c) * rows, rows), :] = heads[c, j, pl.ds(chip * rows, rows), :]
+
+    def take_scores():
+        for c in results:
+            c.wait_recv()
+        results.clear()
+        for j, ref in enumerate((q_ref, k_ref, v_ref)):
+            assemble(j, ref)
+        for head in range(width // HEAD):
+            cols = pl.ds(head * HEAD, HEAD)
+            values_t = v_ref[:, cols].T
+            for step in reversed(range(tokens // block)):
+                n = (step + 1) * block
+                mine_rows = pl.ds(step * block, block)
+                scores = dot(k_ref[pl.ds(0, n), cols], q_ref[mine_rows, cols], 1, 1)
+                scores = scores * (scale * math.log2(math.e))
+                last = jnp.where(below, scores[n - block :], -1e30)
+                scores = last if step == 0 else jnp.concatenate((scores[: n - block], last), axis=0)
+                exps = jnp.exp2(scores - jnp.max(scores, axis=0, keepdims=True))
+                exps = exps * (1.0 / jnp.sum(exps, axis=0, keepdims=True))
+                probs_f[head, pl.ds(0, n), mine_rows] = exps
+                outputs[head, :, mine_rows] = dot(values_t[:, :n], exps.astype(bf16), 1, 0)
+
     landed = set()
 
     def need(names):
@@ -201,6 +235,8 @@
     for name in GATHER:
         if name == "nrm":
             normalize()
+        elif name == "S":
+            take_scores()
         elif name in moves:
             waits, src, dst, to = moves[name]
             need(waits)
@@ -214,17 +250,7 @@
     for c in results:
         c.wait_recv()
 
-    tokens = q_ref.shape[0]
-    block = 512
-    chips = tokens // pair
-    scale = 1.0 / math.sqrt(HEAD)
-    places = [(chip, c) for chip in range(chips) for c in (0, 1)]
-    for j, ref in enumerate((q_ref, k_ref, v_ref, g_ref)):
-        for chip, c in places:
-            ref[pl.ds((2 * chip + c) * rows, rows), :] = heads[c, j, pl.ds(chip * rows, rows), :]
-    below = lax.broadcasted_iota(jnp.int32, (block, block), 0) <= lax.broadcasted_iota(
-        jnp.int32, (block, block), 1
-    )
+    assemble(3, g_ref)
 
     def put(j, chip, c, cols, value):
         for s in range(rows // SLAB):
@@ -235,21 +261,13 @@
     for head in range(width // HEAD):
         cols = pl.ds(head * HEAD, HEAD)
         keys_t = k_ref[:, cols].T
-        values_t = v_ref[:, cols].T
         for step in reversed(range(tokens // block)):
             n = (step + 1) * block
-            mine = pl.ds(step * block, block)
-            query, grad = q_ref[mine, cols], g_ref[mine, cols]
-            scores = dot(k_ref[pl.ds(0, n), cols], query, 1, 1) * (scale * math.log2(math.e))
-            last = jnp.where(below, scores[n - block :], -1e30)
-            scores = last if step == 0 else jnp.concatenate((scores[: n - block], last), axis=0)
-            peak = jnp.max(scores, axis=0, keepdims=True)
-            exps = jnp.exp2(scores - peak)
-            exps = exps * (1.0 / jnp.sum(exps, axis=0, keepdims=True))
-            probs = exps.astype(bf16)
-            output_t = dot(values_t[:, :n], probs, 1, 0)
-            delta = jnp.sum(grad.astype(f32).T * output_t, axis=0, keepdims=True)
+            mine_rows = pl.ds(step * block, block)
+            query, grad = q_ref[mine_rows, cols], g_ref[mine_rows, cols]
+            delta = jnp.sum(grad.astype(f32).T * outputs[head, :, mine_rows], axis=0, keepdims=True)
             grad_probs = dot(v_ref[pl.ds(0, n), cols], grad, 1, 1)
+            exps = probs_f[head, pl.ds(0, n), mine_rows]
             grad_scores = (exps * ((grad_probs - delta) * scale)).astype(bf16)
             grad_query = dot(keys_t[:, :n], grad_scores, 1, 0).T
             for chip, c in places:
@@ -257,7 +275,7 @@
                 if 0 <= offset < block:
                     put(0, chip, c, cols, grad_query[offset : offset + rows])
             more_k = dot(grad_scores, query, 1, 0)
-            more_v = dot(probs, grad, 1, 0)
+            more_v = dot(exps.astype(bf16), grad, 1, 0)
             if step == tokens // block - 1:
                 dk_acc[...] = more_k
                 dv_acc[...] = more_v
@@ -294,63 +312,88 @@
 
     live = {}
 
-    def product(s):
+    def partial(j, s, n, lefts):
         here = pl.ds(s * together, 2 * together)
-
+        cols = pl.ds(pl.multiple_of(n * chunk, chunk), chunk)
+        total = dot(lefts[0, here, :], weights[j, 0, cols, :], 1, 1)
+        for k in (1, 2):
+            total += dot(lefts[k, here, :], weights[j, k, cols, :], 1, 1)
+        return total
+
+    def store(s, n, total):
+        cols = pl.ds(pl.multiple_of(n * chunk, chunk), chunk)
+        part[s : s + 2, :, :, :, cols] = total.astype(bf16).reshape(2, chips // 2, 2, SLAB, chunk)
+
+    def product(s, begin=0):
         def step(n, carry):
-            cols = pl.ds(pl.multiple_of(n * chunk, chunk), chunk)
-            total = dot(back[core, 0, here, :], weights[0, 0, cols, :], 1, 1)
-            for j in (1, 2):
-                total += dot(back[core, j, here, :], weights[0, j, cols, :], 1, 1)
-            for j in (0, 1, 2):
-                total += dot(back_twin[j, here, :], weights[1, j, cols, :], 1, 1)
-            part[s : s + 2, :, :, :, cols] = total.astype(bf16).reshape(2, chips // 2, 2, SLAB, chunk)
+            store(s, n, partial(0, s, n, back.at[core]) + partial(1, s, n, back_twin))
             return carry
 
-        lax.fori_loop(0, depth // chunk, step, 0)
+        lax.fori_loop(begin, depth // chunk, step, 0)
+
+    def own_half():
+        def step(n, carry):
+            own_sums[n] = partial(0, 0, n, back.at[core])
+            return carry
+
+        lax.fori_loop(0, 3, step, 0)
+
+    def first_half(s):
+        def step(n, carry):
+            store(s, n, own_sums[n] + partial(1, s, n, back_twin))
+            return carry
+
+        lax.fori_loop(0, 3, step, 0)
 
     early, latter = pl.ds(0, wide), pl.ds(wide, wide)
 
-    def first(s):
+    whole = pl.ds(0, depth)
+
+    def first(s, cols):
+        def lay(key, src, dst, to):
+            live.setdefault(key, []).append(go(src.at[all_rows, cols], dst.at[all_rows, cols], to))
+
         if s in ACROSS_FIRST:
             for r in (2, 1, 3, 0):
-                live["za", s, r] = go(part.at[s, spot(r), other], za.at[r], across)
+                lay(("za", s, r), part.at[s, spot(r), other], za.at[r], across)
             return
-        live["x1r", s] = go(part.at[s, spot(2), 0], xb1.at[s, 0], right)
-        live["x1l", s] = go(part.at[s, spot(2), 1], xb1.at[s, 1], left)
-        live["x2", s] = [
-            go(part.at[s, spot(1), 1], xb2.at[s, 0, 1], right),
-            go(part.at[s, spot(3), 0], xb2.at[s, 1, 0], left),
-        ]
+        lay(("x1r", s), part.at[s, spot(2), 0], xb1.at[s, 0], right)
+        lay(("x1l", s), part.at[s, spot(2), 1], xb1.at[s, 1], left)
+        lay(("x2", s), part.at[s, spot(1), 1], xb2.at[s, 0, 1], right)
+        lay(("x2", s), part.at[s, spot(3), 0], xb2.at[s, 1, 0], left)
+
+    def arrive(*key):
+        for c in live[key]:
+            c.wait_recv()
 
     def second(s):
         if s in ACROSS_FIRST:
             two, one, three = (part.at[s, spot(r), z] for r in (2, 1, 3))
-            live["za", s, 2].wait_recv()
+            arrive("za", s, 2)
             plus(two, za.at[2])
-            live["x1r", s] = go(two.at[all_rows, early], xb1.at[s, 0, all_rows, early], right)
-            live["x1l", s] = go(two.at[all_rows, latter], xb1.at[s, 0, all_rows, latter], left)
-            live["za", s, 1].wait_recv()
+            live["x1r", s] = [go(two.at[all_rows, early], xb1.at[s, 0, all_rows, early], right)]
+            live["x1l", s] = [go(two.at[all_rows, latter], xb1.at[s, 0, all_rows, latter], left)]
+            arrive("za", s, 1)
             plus(one, za.at[1])
             live["x2", s] = [go(one.at[all_rows, latter], xb2.at[s, 0, 0, all_rows, latter], right)]
-            live["za", s, 3].wait_recv()
+            arrive("za", s, 3)
             plus(three, za.at[3])
             live["x2", s].append(go(three.at[all_rows, early], xb2.at[s, 1, 0, all_rows, early], left))
             return
-        live["x1r", s].wait_recv()
+        arrive("x1r", s)
         plus(part.at[s, spot(1), 0], xb1.at[s, 0])
         live["x2", s].append(go(part.at[s, spot(1), 0], xb2.at[s, 0, 0], right))
-        live["x1l", s].wait_recv()
+        arrive("x1l", s)
         plus(part.at[s, spot(3), 1], xb1.at[s, 1])
         live["x2", s].append(go(part.at[s, spot(3), 1], xb2.at[s, 1, 1], left))
 
     def cross(s):
         if s in ACROSS_FIRST:
             one, three = (part.at[s, spot(r), z] for r in (1, 3))
-            live["x1r", s].wait_recv()
+            arrive("x1r", s)
             plus(one.at[all_rows, early], xb1.at[s, 0, all_rows, early])
             live["x2", s].append(go(one.at[all_rows, early], xb2.at[s, 0, 0, all_rows, early], right))
-            live["x1l", s].wait_recv()
+            arrive("x1l", s)
             plus(three.at[all_rows, latter], xb1.at[s, 0, all_rows, latter])
             live["x2", s].append(go(three.at[all_rows, latter], xb2.at[s, 1, 0, all_rows, latter], left))
             return
@@ -363,8 +406,8 @@
     def norm_back(s):
         here = pl.ds(s * SLAB, SLAB)
         if s in ACROSS_FIRST:
-            for c in live["x2", s] + [live["za", s, 0]]:
-                c.wait_recv()
+            arrive("x2", s)
+            arrive("za", s, 0)
         else:
             live["z", s].wait_recv()
         saved = saved_ref[here, :].astype(f32)
@@ -449,11 +492,14 @@
             updated_ref[here, cols] = total.astype(bf16)
 
     stages = {
-        "product": product, "first": first, "second": second, "across": cross, "norm": norm_back,
+        "product": product, "producta": first_half, "productb": lambda s: product(s, 3),
+        "first": lambda s: first(s, whole), "firsta": lambda s: first(s, early),
+        "firstb": lambda s: first(s, latter), "second": second, "across": cross, "norm": norm_back,
         "relay_y": lambda s: relay(s, 0), "relay_z": lambda s: relay(s, 1),
         "sums_y": lambda s: sums(s, 0), "sums_z": lambda s: sums(s, 1),
         "late_y": lambda s: late(s, 0), "late_z": lambda s: late(s, 1), "finish": finish,
     }
+    own_half()
     for c in swaps:
         c.wait_recv()
     for name in SUMS:
@@ -494,8 +540,11 @@
             buffer(tokens, width),
             buffer(tokens, width),
             buffer(tokens, width),
+            pltpu.VMEM((width // HEAD, tokens, tokens), f32),
+            pltpu.VMEM((width // HEAD, HEAD, tokens), f32),
             pltpu.VMEM((tokens, HEAD), f32),
             pltpu.VMEM((tokens, HEAD), f32),
+            pltpu.VMEM((3, 4 * rows, 512), f32),
             buffer(2, 3, tokens // 2, width),
             buffer(3, tokens // 2, width),
             buffer(slabs, 4, 2, SLAB, depth),
@@ -508,12 +557,12 @@
             buffer(slabs, 2, 3, SLAB, wide),
             buffer(slabs, 2, 3, SLAB, wide),
             pltpu.VMEM((slabs, 2, SLAB, wide), f32),
-            pltpu.SemaphoreType.DMA((43 + 27 * slabs,)),
-            pltpu.SemaphoreType.DMA((43 + 27 * slabs,)),
+            pltpu.SemaphoreType.DMA((48 + 28 * slabs,)),
+            pltpu.SemaphoreType.DMA((48 + 28 * slabs,)),
             pltpu.SemaphoreType.DMA((9,)),
         ],
         compiler_params=pltpu.CompilerParams(
-            collective_id=1, has_side_effects=True, vmem_limit_bytes=56 * 2**20
+            collective_id=1, has_side_effects=True, vmem_limit_bytes=59 * 2**20
         ),
         cost_estimate=pl.CostEstimate(flops=14 * 10**9, bytes_accessed=10**7, transcendentals=10**6),
     )(*(pltpu.with_memory_space_constraint(a, pltpu.HBM) for a in (

time: 122 us -> 123 us (level); the launches traced: 121 us -> 120 us
    pallas_call x1, Pallas kernels: 119 us -> 118 us  [on_device(): pl.pallas_call(kernel, out_shape=(rows_out, rows_out), in_specs=[hbm] * 9...]
where the time goes in v5:
time: 123 us; the launch traced here: 120 us
  Pallas kernels  118 us (96%)
  local copies, waits for them, and re-layouts  1.49 us (1%)
    pallas_call x1, Pallas kernels, on_device(): pl.pallas_call(kernel, out_shape=(rows_out, rows_out), in_specs=[hbm] * 9...  118 us

profile of v5, /device:TPU:8, one launch (start us, length us, event | category | flops | bytes accessed | tf_op | source)
XLA Modules:
  0.0 120.1 jit_solution(1191676626933590708)
XLA Ops:
  0.6 118.0 %shard_map.104 = (bf16[64,3072]{1,0:T(8,128)(2,1)S(1)}, bf16[64,3072]{1,0:T(8,128)(2,1)S(1)}) custom-call(f32[16,16]{1,0:T(8,128)} %alpha_in.1, bf16[64,3072]{1,0:T(8,128)(2,1)} %bitcast.15, f32[1,3072]{1,0:T(1,128)} %gain_in.1, bf16[64,3072]{1,0:T(8,128)(2,1)} %bitcast.16, bf16[64,3072]{1,0:T(8,128)(2,1)} %bitcast.17, bf16[3072,256]{1,0:T(8,128)(2,1)} %bitcast.11, ...), custom_call_target="tpu_custom_call" | custom-call | flops 14000000000 | bytes 10000000 | tf_op jit(solution)/shard_map/pallas_call | solution.py:524
  118.6 0.7 copy.13
  119.3 0.7 copy.14

commit v6 on v5

--- a/solution.py
+++ b/solution.py
@@ -18,15 +18,15 @@
 GATHER = (
     "gLlo", "gRlo", "gA", "nrm", "nRhi", "gLhi", "nLlo", "gxR", "nLhi", "nA", "nRlo", "gxL", "gRhi",
     "g3A", "oRlo", "oLhi", "P0t", "P0", "oRhi", "oLlo", "g1A", "G0", "G3", "oxL", "nxR", "oxR",
-    "P1t", "g2Ahi", "P3t", "nxL", "P3", "P1", "g2Alo", "G1", "zxR", "zxL", "P2t", "P2", "G2", "S",
+    "P1t", "g2Ahi", "P3t", "nxL", "P3", "P1", "g2Alo", "G1", "zxR", "zxL", "P2t", "P2", "S", "G2",
 )
 SUMS = (
-    "producta0", "firsta0", "firsta1", "productb0", "firstb0", "firstb1", "product2", "second1",
-    "second0", "across1", "across0", "first2", "norm1", "relay_y1", "norm0", "first3", "sums_y1",
-    "relay_z1", "relay_y0", "second2", "sums_y0", "relay_z0", "second3", "across2", "across3",
-    "sums_z1", "norm2", "norm3", "sums_z0", "relay_z2", "relay_y2", "late_z1", "late_y0",
-    "relay_z3", "relay_y3", "sums_y2", "sums_z2", "sums_y3", "late_z0", "sums_z3", "late_y2",
-    "late_y1", "late_z2", "late_y3", "finish0", "late_z3", "finish1", "finish2", "finish3",
+    "producta0", "firsta1", "firsta0", "productb0", "firstb0", "firstb1", "product2", "second1",
+    "across1", "second0", "across0", "norm1", "first2", "norm0", "relay_z1", "relay_y1", "first3",
+    "relay_y0", "sums_y1", "second2", "relay_z0", "sums_z1", "sums_y0", "second3", "across2",
+    "sums_z0", "late_z1", "across3", "norm2", "late_z0", "norm3", "relay_z2", "relay_y3",
+    "relay_y2", "late_y1", "relay_z3", "sums_y3", "sums_z2", "sums_y2", "sums_z3", "finish1",
+    "late_y3", "late_y0", "late_z2", "late_y2", "late_z3", "finish0", "finish3", "finish2",
 )
 ACROSS_FIRST = (0,)
 
@@ -502,10 +502,15 @@
     own_half()
     for c in swaps:
         c.wait_recv()
+    def settle(keep):
+        while len(sends) > keep:
+            sends.pop(0).wait_send()
+
     for name in SUMS:
+        if name[:-1] in ("second", "norm", "finish"):
+            settle(30)
         stages[name[:-1]](int(name[-1]))
-    for c in sends:
-        c.wait_send()
+    settle(0)
 
 
 def on_device(saved_in, out_grad, pending, gain, alpha, w_query, w_key, w_value, w_out):

time: 123 us -> 120 us (0.976); the launches traced: 120 us -> 119 us
  no operation moved by 1% of the time
where the time goes in v6:
time: 120 us; the launch traced here: 119 us
  Pallas kernels  117 us (98%)
  local copies, waits for them, and re-layouts  1.49 us (1%)
    pallas_call x1, Pallas kernels, on_device(): pl.pallas_call(kernel, out_shape=(rows_out, rows_out), in_specs=[hbm] * 9...  117 us

profile of v6, /device:TPU:8, one launch (start us, length us, event | category | flops | bytes accessed | tf_op | source)
XLA Modules:
  0.0 119.3 jit_solution(10051058331706486018)
XLA Ops:
  0.6 117.2 %shard_map.104 = (bf16[64,3072]{1,0:T(8,128)(2,1)S(1)}, bf16[64,3072]{1,0:T(8,128)(2,1)S(1)}) custom-call(f32[16,16]{1,0:T(8,128)} %alpha_in.1, bf16[64,3072]{1,0:T(8,128)(2,1)} %bitcast.15, f32[1,3072]{1,0:T(1,128)} %gain_in.1, bf16[64,3072]{1,0:T(8,128)(2,1)} %bitcast.16, bf16[64,3072]{1,0:T(8,128)(2,1)} %bitcast.17, bf16[3072,256]{1,0:T(8,128)(2,1)} %bitcast.11, ...), custom_call_target="tpu_custom_call" | custom-call | flops 14000000000 | bytes 10000000 | tf_op jit(solution)/shard_map/pallas_call | solution.py:529
  117.8 0.7 copy.13
  118.6 0.7 copy.14

commit v7 on v6

--- a/solution.py
+++ b/solution.py
@@ -99,6 +99,17 @@
     friends = (right, left, across, twin) + up + down
     for friend in friends:
         pl.semaphore_signal(barrier, inc=1, device_id=friend, device_id_type=MESH)
+    for c in load_rows:
+        c.wait()
+
+    def one(i, carry):
+        here = pl.ds(pl.multiple_of(i * 16, 16), 16)
+        values = saved_ref[here, :].astype(f32)
+        factor = lax.rsqrt(jnp.mean(values * values, axis=-1, keepdims=True) + eps)
+        normed[0, z, here, :] = (values * factor * gain_ref[...]).astype(bf16)
+        return carry
+
+    lax.fori_loop(0, rows // 16, one, 0)
     pl.semaphore_wait(barrier, len(friends))
 
     w_twin = []
@@ -106,18 +117,7 @@
     quarter = [pl.ds(i * SLAB, SLAB) for i in range(rows // SLAB)]
     sent = {}
 
-    def normalize():
-        for c in load_rows:
-            c.wait()
-
-        def one(i, carry):
-            here = pl.ds(pl.multiple_of(i * 16, 16), 16)
-            values = saved_ref[here, :].astype(f32)
-            factor = lax.rsqrt(jnp.mean(values * values, axis=-1, keepdims=True) + eps)
-            normed[0, z, here, :] = (values * factor * gain_ref[...]).astype(bf16)
-            return carry
-
-        lax.fori_loop(0, rows // 16, one, 0)
+    def trade_weights():
         for j, w in enumerate((wq_ref, wk_ref, wv_ref)):
             w_twin.append(go(w, weights.at[1, j], twin))
         w_twin.append(go(wo_ref, out_weights.at[1], twin))
@@ -234,7 +234,7 @@
 
     for name in GATHER:
         if name == "nrm":
-            normalize()
+            trade_weights()
         elif name == "S":
             take_scores()
         elif name in moves:

time: 120 us -> 122 us (1.017)
  no operation moved by 1% of the time
where the time goes in v7:
time: 122 us; the launch traced here: 120 us
  Pallas kernels  118 us (97%)
  local copies, waits for them, and re-layouts  1.49 us (1%)
    pallas_call x1, Pallas kernels, on_device(): pl.pallas_call(kernel, out_shape=(rows_out, rows_out), in_specs=[hbm] * 9...  118 us

profile of v7, /device:TPU:8, one launch (start us, length us, event | category | flops | bytes accessed | tf_op | source)
XLA Modules:
  0.0 120.3 jit_solution(16858082106704504254)
XLA Ops:
  0.6 118.1 %shard_map.104 = (bf16[64,3072]{1,0:T(8,128)(2,1)S(1)}, bf16[64,3072]{1,0:T(8,128)(2,1)S(1)}) custom-call(f32[16,16]{1,0:T(8,128)} %alpha_in.1, bf16[64,3072]{1,0:T(8,128)(2,1)} %bitcast.15, f32[1,3072]{1,0:T(1,128)} %gain_in.1, bf16[64,3072]{1,0:T(8,128)(2,1)} %bitcast.16, bf16[64,3072]{1,0:T(8,128)(2,1)} %bitcast.17, bf16[3072,256]{1,0:T(8,128)(2,1)} %bitcast.11, ...), custom_call_target="tpu_custom_call" | custom-call | flops 14000000000 | bytes 10000000 | tf_op jit(solution)/shard_map/pallas_call | solution.py:529
  118.8 0.7 copy.13
  119.5 0.7 copy.14
